TPU v7x, 32 devices: a whole 2x2x4 slice. The times are simulated.
32 devices in a mesh: section: 2 (over x), owner: 4 (over z), context: 4 (over y, core).
Axes of the slice: x: 2, y: 2, z: 4, core: 2. Of those that a mesh axis runs over, the one named last changes fastest.
Arguments:
- x_attn: bfloat16 [16384, 8192], P(('section', 'context'), 'owner'), parts along dimension 0, may hold values from -6 to 6
- x_mlp: bfloat16 [16384, 8192], P(('section', 'context'), 'owner'), parts along dimension 0, may hold values from -6 to 6
- x_down: bfloat16 [16384, 29568], P(('section', 'context'), 'owner'), parts along dimension 0, may hold values from -6 to 6
- omega_attn: bfloat16 [16384, 256], P(('section', 'owner')), parts along dimension 0, may hold values from -6 to 6
- omega_mlp: bfloat16 [16384, 256], P(('section', 'owner')), parts along dimension 0, may hold values from -6 to 6
- omega_down: bfloat16 [59136, 256], P(('section', 'owner')), parts along dimension 0, may hold values from -6 to 6
- basis_attn: bfloat16 [16384, 256], P(('section', 'owner')), parts along dimension 0, may hold values from -1 to 1
- basis_mlp: bfloat16 [16384, 256], P(('section', 'owner')), parts along dimension 0, may hold values from -1 to 1
- basis_down: bfloat16 [59136, 256], P(('section', 'owner')), parts along dimension 0, may hold values from -1 to 1
- eig_attn: float32 [512], P('section'), parts along dimension 0, may hold values from 2 to 20
- eig_mlp: float32 [512], P('section'), parts along dimension 0, may hold values from 2 to 20
- eig_down: float32 [512], P('section'), parts along dimension 0, may hold values from 2 to 20
Outputs:
- sketch_attn: float32 [16384, 256], P(('section', 'owner', 'context')), parts along dimension 0
- sketch_mlp: float32 [16384, 256], P(('section', 'owner', 'context')), parts along dimension 0
- sketch_down: float32 [59136, 256], P(('section', 'owner', 'context')), parts along dimension 0
There are 2 independent parts, one for each index of `section`. A program takes and returns all parts, laid end to end along the dimension named above; each array names one. Nothing has to cross between parts.
All inputs are finite; a program needn't handle non-finite values.
Results may differ from a plain program's by a relative error of at most 0.0003.
Values may be sent and summed in bfloat16 or wider, within the bound.
No kernel may reach another device: no remote copies, remote signals or barrier semaphores. Data moves between devices by JAX's collectives and lax.ppermute only.
A program may use at most 128 MiB of HBM per device.

v0:
```python
import jax
import jax.numpy as jnp
from jax import lax
from jax.sharding import PartitionSpec as P


def token_contract(inputs, probe):
    return lax.dot_general(
        inputs, probe, (((0,), (0,)), ((), ())), preferred_element_type=jnp.float32
    )


def prior_rows(basis, eigen, core):
    rows = basis.shape[0] // lax.axis_size("context")
    picked = lax.dynamic_slice_in_dim(basis, lax.axis_index("context") * rows, rows, 0)
    weighted = eigen[:, None] * core
    return 0.9 * jnp.dot(picked.astype(jnp.float32), weighted, precision=lax.Precision.HIGHEST)


def factor_share(inputs, probe):
    return lax.psum_scatter(
        token_contract(inputs, probe), "context", scatter_dimension=0, tiled=True
    )


def per_device(
    x_attn,
    x_mlp,
    x_down,
    omega_attn,
    omega_mlp,
    omega_down,
    basis_attn,
    basis_mlp,
    basis_down,
    eig_attn,
    eig_mlp,
    eig_down,
):
    inputs = (x_attn, x_mlp, x_down)
    omegas = (omega_attn, omega_mlp, omega_down)
    bases = (basis_attn, basis_mlp, basis_down)
    eigens = (eig_attn, eig_mlp, eig_down)
    total = x_attn.shape[0] * lax.axis_size("context")
    probes_local = [
        jnp.dot(x, w, preferred_element_type=jnp.float32) for x, w in zip(inputs, omegas)
    ]
    cores_local = [token_contract(b, w) for b, w in zip(bases, omegas)]
    summed = lax.psum(
        (
            probes_local[0],
            probes_local[1],
            probes_local[2],
            cores_local[0],
            cores_local[1],
            cores_local[2],
        ),
        "owner",
    )
    cores = summed[3:]
    datas = [factor_share(x, z.astype(jnp.bfloat16)) for x, z in zip(inputs, summed[:3])]
    results = [
        prior_rows(b, e, c) + 0.1 / total * d for b, e, c, d in zip(bases, eigens, cores, datas)
    ]
    return (results[0], results[1], results[2])


def solution(mesh):
    placed = (
        P(("section", "context"), "owner"),
        P(("section", "context"), "owner"),
        P(("section", "context"), "owner"),
        P(("section", "owner"), None),
        P(("section", "owner"), None),
        P(("section", "owner"), None),
        P(("section", "owner"), None),
        P(("section", "owner"), None),
        P(("section", "owner"), None),
        P("section"),
        P("section"),
        P("section"),
    )
    return jax.shard_map(
        per_device,
        mesh=mesh,
        in_specs=placed,
        out_specs=(
            P(("section", "owner", "context"), None),
            P(("section", "owner", "context"), None),
            P(("section", "owner", "context"), None),
        ),
        check_vma=False,
    )
```

profile of v0, /device:TPU:0, one launch (start us, length us, event | category | flops | bytes accessed | tf_op | source)
XLA Modules:
  0.0 428.3 jit_solution(12112903417987098611)
XLA Ops:
  8.0 0.0 all-reduce.5.cloned.1.call-start
  8.1 1.2 copy-done
  9.2 2.5 fusion.18
  11.8 2.7 fusion.20
  14.5 4.0 fusion.22
  18.5 0.0 reduce-scatter.4.cloned.1.call-start
  18.6 5.8 %fusion.19 = f32[2048,256]{1,0:T(8,128)S(1)} fusion(bf16[2048,2048]{1,0:T(8,128)(2,1)} %param.12, bf16[2048,256]{1,0:T(8,128)(2,1)S(1)} %copy-done), kind=kOutput, calls=%fused_computation.25 | convolution fusion | flops 2147483648 | bytes 11534336 | tf_op jit(solution)/shard_map/dot_general | solution.py:46
  24.4 7.4 %fusion.21 = f32[2048,256]{1,0:T(8,128)} fusion(bf16[2048,2048]{1,0:T(8,128)(2,1)} %param.13, bf16[2048,256]{1,0:T(8,128)(2,1)S(1)} %copy-done.2), kind=kOutput, calls=%fused_computation.27 | convolution fusion | flops 2147483648 | bytes 11534336 | tf_op jit(solution)/shard_map/dot_general | solution.py:46
  31.8 15.4 %fusion.23 = f32[2048,256]{1,0:T(8,128)} fusion(bf16[2048,7392]{0,1:T(8,128)(2,1)} %param.14, bf16[7392,256]{1,0:T(8,128)(2,1)S(1)} %copy-done.7), kind=kOutput, calls=%fused_computation.29 | convolution fusion | flops 7751073792 | bytes 36159488 | tf_op jit(solution)/shard_map/dot_general | solution.py:46
  47.2 225.2 %all-reduce.6 = (bf16[2048,256]{1,0:T(8,128)(2,1)}, bf16[2048,256]{1,0:T(8,128)(2,1)}, bf16[2048,256]{1,0:T(8,128)(2,1)S(1)}) all-reduce(f32[2048,256]{1,0:T(8,128)S(1)} %fusion.19, f32[2048,256]{1,0:T(8,128)} %fusion.21, f32[2048,256]{1,0:T(8,128)} %fusion.23), channel_id=1, replica_groups=mesh['section'=2,'owner'=4,'context'=4] {'owner'}, use_global_device_ids=true, to_apply=%region_1.0 | all-reduce | flops 1572864 | bytes 9437184 | tf_op jit(solution)/shard_map/psum | solution.py:49
  272.4 8.6 %convolution_bitcast_fusion.2 = f32[2048,256]{1,0:T(8,128)} fusion(bf16[2048,2048]{1,0:T(8,128)(2,1)} %param.12, bf16[2048,256]{1,0:T(8,128)(2,1)} %get-tuple-element.3), kind=kOutput, calls=%fused_computation.4 | convolution fusion | flops 2147483648 | bytes 11534336 | tf_op jit(solution)/shard_map/dot_general | solution.py:8
  281.0 0.0 reduce-scatter.4.cloned.1.call-update
  281.0 0.0 reduce-scatter.6.cloned.1.call-start
  281.0 8.1 %convolution_bitcast_fusion.1 = f32[2048,256]{1,0:T(8,128)} fusion(bf16[2048,2048]{1,0:T(8,128)(2,1)} %param.13, bf16[2048,256]{1,0:T(8,128)(2,1)S(1)} %copy-done.8), kind=kOutput, calls=%fused_computation.3 | convolution fusion | flops 2147483648 | bytes 11534336 | tf_op jit(solution)/shard_map/dot_general | solution.py:8
  289.1 0.0 reduce-scatter.6.cloned.1.call-update
  289.1 0.3 reduce-scatter.8.cloned.1.call-start
  289.4 16.2 %convolution_bitcast_fusion = f32[7392,256]{1,0:T(8,128)} fusion(bf16[2048,7392]{0,1:T(8,128)(2,1)} %param.14, bf16[2048,256]{1,0:T(8,128)(2,1)S(1)} %get-tuple-element.5), kind=kOutput, calls=%fused_computation | convolution fusion | flops 7751073792 | bytes 38895616 | tf_op jit(solution)/shard_map/dot_general | solution.py:8
  305.6 0.0 all-reduce.5.cloned.1.call-done
  305.6 7.6 %reduce-scatter.4.cloned.1.call-done = f32[512,256]{1,0:T(8,128)} async-done(((f32[2048,256]{1,0:T(8,128)}), f32[512,256]{1,0:T(8,128)}) %reduce-scatter.4.cloned.1.call-update) | async-done | bytes 524304 | tf_op jit(solution)/shard_map/reduce_scatter | solution.py:21
  313.2 2.6 fusion.2
  315.8 31.4 %reduce-scatter.6.cloned.1.call-done = f32[512,256]{1,0:T(8,128)} async-done(((f32[2048,256]{1,0:T(8,128)}), f32[512,256]{1,0:T(8,128)}) %reduce-scatter.6.cloned.1.call-update) | async-done | bytes 524304 | tf_op jit(solution)/shard_map/reduce_scatter | solution.py:21
  347.1 2.5 fusion.1
  349.6 66.9 %reduce-scatter.8.cloned.1.call-done = f32[1848,256]{1,0:T(8,128)} async-done(((f32[7392,256]{1,0:T(8,128)}), f32[1848,256]{1,0:T(8,128)}) %reduce-scatter.8.cloned.1.call-update) | async-done | bytes 1892368 | tf_op jit(solution)/shard_map/reduce_scatter | solution.py:21
  416.5 4.2 fusion
  (19 shorter events, 0.1 us)
Async XLA Ops:
  8.0 1.2 copy-start
  8.0 297.6 %all-reduce.5.cloned.1.call-start = ((), (), s32[]{:S(2)}) async-start(), calls=%async_computation.6 | async-start | bytes 1572864 | tf_op jit(solution)/shard_map/psum | solution.py:49
  9.2 5.3 %copy-start.3 = (bf16[7392,256]{1,0:T(8,128)(2,1)S(1)}, bf16[7392,256]{1,0:T(8,128)(2,1)}, u32[]{:S(2)}) copy-start(bf16[7392,256]{1,0:T(8,128)(2,1)} %param.20) | copy-start | bytes 11354116
  18.5 294.7 %reduce-scatter.4.cloned.1.call-start = ((), (), s32[]{:S(2)}) async-start(), calls=%async_computation.3 | async-start | bytes 2621440 | tf_op jit(solution)/shard_map/reduce_scatter | solution.py:21
  18.6 5.8 %copy-start.2 = (bf16[2048,256]{1,0:T(8,128)(2,1)S(1)}, bf16[2048,256]{1,0:T(8,128)(2,1)}, u32[]{:S(2)}) copy-start(bf16[2048,256]{1,0:T(8,128)(2,1)} %param.16) | copy-start | bytes 3145732
  24.4 7.4 %copy-start.7 = (bf16[7392,256]{1,0:T(8,128)(2,1)S(1)}, bf16[7392,256]{1,0:T(8,128)(2,1)}, u32[]{:S(2)}) copy-start(bf16[7392,256]{1,0:T(8,128)(2,1)} %param.17) | copy-start | bytes 11354116
  272.4 8.6 %copy-start.8 = (bf16[2048,256]{1,0:T(8,128)(2,1)S(1)}, bf16[2048,256]{1,0:T(8,128)(2,1)}, u32[]{:S(2)}) copy-start(bf16[2048,256]{1,0:T(8,128)(2,1)} %get-tuple-element.4) | copy-start | bytes 3145732
  281.0 66.1 %reduce-scatter.6.cloned.1.call-start = ((), (), s32[]{:S(2)}) async-start(), calls=%async_computation.4 | async-start | bytes 2621440 | tf_op jit(solution)/shard_map/reduce_scatter | solution.py:21
  289.1 127.4 %reduce-scatter.8.cloned.1.call-start = ((), (), s32[]{:S(2)}) async-start(), calls=%async_computation.5 | async-start | bytes 9461760 | tf_op jit(solution)/shard_map/reduce_scatter | solution.py:21
  305.6 7.6 %copy-start.4 = (f32[256]{0:T(256)S(1)}, f32[256]{0:T(256)}, u32[]{:S(2)}) copy-start(f32[256]{0:T(256)} %param.21) | copy-start | bytes 3076
  305.6 41.6 %copy-start.5 = (f32[256]{0:T(256)S(1)}, f32[256]{0:T(256)}, u32[]{:S(2)}) copy-start(f32[256]{0:T(256)} %param.22) | copy-start | bytes 3076
  305.6 110.9 %copy-start.6 = (f32[256]{0:T(256)S(1)}, f32[256]{0:T(256)}, u32[]{:S(2)}) copy-start(f32[256]{0:T(256)} %param.23) | copy-start | bytes 3076
  313.2 107.5 %copy-start.1 = (bf16[2048,256]{1,0:T(8,128)(2,1)S(1)}, bf16[2048,256]{1,0:T(8,128)(2,1)}, u32[]{:S(2)}) copy-start(bf16[2048,256]{1,0:T(8,128)(2,1)} %param.15) | copy-start | bytes 3145732
Sparse Core Ops, SparseCore 0:
  18.6 56.0 all-reduce.4
Sparse Core Ops, SparseCore 1:
  281.1 32.1 reduce-scatter.3
  315.8 31.3 reduce-scatter.5
  349.6 66.9 reduce-scatter.7
where the time goes:
time: 429 us; the launch traced here: 428 us
  blocking collectives  225 us (52%)
  waiting for transfers between devices  106 us (25%)
  matrix products  79.8 us (19%)
  between operations  15.7 us (4%)
    psum x1, blocking collectives, per_device(): lax.psum((probes_local[0], probes_local[1], probes_local[2], cores_local[...  225 us
    reduce_scatter x3, waiting for transfers between devices, factor_share(): lax.psum_scatter(token_contract(inputs, probe), 'context', scatter_dimens...  106 us
    dot_general x6, matrix products, token_contract(): lax.dot_general(inputs, probe, (((0,), (0,)), ((), ())), preferred_elemen...  42 us
    dot_general x3, matrix products, per_device(): jnp.dot(x, w, preferred_element_type=jnp.float32)  28.6 us
    dot_general x3, matrix products, prior_rows(): jnp.dot(picked.astype(jnp.float32), weighted, precision=lax.Precision.HIG...  9.21 us
  transfers between devices with their start and end apart: 4, of which 3 were waited for; matrix products, arithmetic and copies ran while one was open for 16% of the time, Pallas kernels for 0%

commit v1 on v0

v1 whole, which is shorter than its diff:
```python
import functools

import jax
import jax.numpy as jnp
from jax import lax
from jax.experimental import pallas as pl
from jax.experimental.pallas import tpu as pltpu
from jax.sharding import PartitionSpec as P

INWARD = ((0, 1), (3, 2))
ACROSS = ((1, 2), (2, 1))
OUTWARD = ((1, 0), (2, 3))
PAIRED = ((0, 1), (1, 0), (2, 3), (3, 2))
SKIPPED = ((0, 2), (2, 0), (1, 3), (3, 1))
CHUNKS = 2
CARRIER = 2
MIB = 1024 * 1024
FIRST = (((0,), (0,)), ((), ()))
ANYWHERE = pl.BlockSpec(memory_space=pl.ANY)


def token_contract(inputs, probe):
    return lax.dot_general(inputs, probe, FIRST, preferred_element_type=jnp.float32)


def prior_rows(basis, eigen, core):
    rows = basis.shape[0] // lax.axis_size("context")
    picked = lax.dynamic_slice_in_dim(basis, lax.axis_index("context") * rows, rows, 0)
    weighted = eigen[:, None] * core
    return 0.9 * jnp.dot(picked.astype(jnp.float32), weighted, precision=lax.Precision.HIGHEST)


def core_total(bases, omegas):
    size = lax.axis_size("context")
    rank = omegas[0].shape[1]
    share = rank // size
    start = lax.axis_index("context") * share
    mine = [
        token_contract(lax.dynamic_slice_in_dim(b, start, share, 1), w)
        for b, w in zip(bases, omegas)
    ]
    summed = lax.psum(jnp.concatenate(mine, 0), "owner")
    whole = lax.all_gather(summed, "context", axis=0)
    whole = whole.reshape(size, len(bases), share, rank)
    return [whole[:, k].reshape(rank, rank) for k in range(len(bases))]


class Order:
    def __init__(self):
        self.last = ()

    def call(self, kernel, operands, out, after=(), vmem=8 * MIB, **rest):
        held = (*self.last, *after)
        count = len(operands)

        def body(*refs):
            kernel(*refs[:count], *refs[count + len(held) :])

        specs = rest.pop("in_specs", [pl.BlockSpec(memory_space=pltpu.VMEM)] * count)
        result = pl.pallas_call(
            body,
            out_shape=out,
            in_specs=[*specs, *[ANYWHERE] * len(held)],
            cost_estimate=pl.CostEstimate(flops=1000, bytes_accessed=1000, transcendentals=0),
            compiler_params=pltpu.CompilerParams(vmem_limit_bytes=vmem),
            **rest,
        )(*operands, *held)
        self.last = (result[-1] if isinstance(result, (tuple, list)) else result,)
        return result


def probe_rows(order, inputs, omega, start, rows, turned):
    tile = 512
    rank = omega.shape[1]
    first = start // tile

    def kernel(x, w, out):
        if turned:
            out[...] = token_contract(x[...], w[...])
        else:
            out[...] = jnp.dot(x[...], w[...], preferred_element_type=jnp.float32)

    depth = omega.shape[0]
    if turned:
        spec = pl.BlockSpec((depth, tile), lambda i: (0, first + i))
    else:
        spec = pl.BlockSpec((tile, depth), lambda i: (first + i, 0))
    return order.call(
        kernel,
        (inputs, omega),
        jax.ShapeDtypeStruct((rows, rank), jnp.float32),
        vmem=44 * MIB,
        grid=(rows // tile,),
        in_specs=[spec, pl.BlockSpec((depth, rank), lambda i: (0, 0))],
        out_specs=pl.BlockSpec((tile, rank), lambda i: (i, 0)),
    )


def paired(order, partial, arrived, after):
    half = partial.shape[0] // 2

    def kernel(mine, theirs, kept, given):
        here = lax.select(lax.axis_index("owner") < 2, 0, half)
        near = pl.ds(pl.multiple_of(here, half), half)
        away = pl.ds(pl.multiple_of(half - here, half), half)
        given[...] = mine[away, :] + theirs[away, :]
        kept[...] = mine[near, :] + theirs[near, :]

    shape = jax.ShapeDtypeStruct((half, partial.shape[1]), jnp.float32)
    return order.call(kernel, (partial, arrived), (shape, shape), after)


def rounded(order, kept, arrived, exact):
    rows, rank = kept.shape
    plain = rows - exact

    def kernel(mine, theirs, out):
        total = mine[...] + theirs[...]
        out[:plain, :] = total[:plain].astype(jnp.bfloat16)
        rest = total[plain:]
        for i in range(3 if exact else 0):
            term = rest.astype(jnp.bfloat16)
            out[plain + i * exact : plain + (i + 1) * exact, :] = term
            rest = rest - term.astype(jnp.float32)

    shape = jax.ShapeDtypeStruct((plain + 3 * exact, rank), jnp.bfloat16)
    return order.call(kernel, (kept, arrived), shape)


def data_rows(order, inputs, probe, turned):
    features = inputs.shape[0] if turned else inputs.shape[1]
    tokens, rank = probe.shape
    tile = features // 4 if turned else features // 2

    def kernel(x, p, out):
        if turned:
            out[...] = jnp.dot(x[...], p[...], preferred_element_type=jnp.float32)
        else:
            out[...] = token_contract(x[...], p[...])

    if turned:
        tile = -(-features // 64) * 16
        spec = pl.BlockSpec((tile, tokens), lambda i: (i, 0))
    else:
        spec = pl.BlockSpec((tokens, tile), lambda i: (0, i))
    return order.call(
        kernel,
        (inputs, probe),
        jax.ShapeDtypeStruct((features, rank), jnp.float32),
        vmem=44 * MIB,
        grid=(pl.cdiv(features, tile),),
        in_specs=[spec, pl.BlockSpec((tokens, rank), lambda i: (0, 0))],
        out_specs=pl.BlockSpec((tile, rank), lambda i: (i, 0)),
    )


def halves(data, other):
    quarters = data.reshape(2, 2, data.shape[0] // 4, data.shape[1])
    return lax.dynamic_index_in_dim(quarters, other, 1, keepdims=False)


def core_summed(order, kept, arrived):
    def kernel(mine, theirs, stays, given):
        high = lax.select(lax.axis_index("context") >= 2, 1, 0)
        given[...] = mine[1 - high] + theirs[1 - high]
        stays[...] = mine[high] + theirs[high]

    shape = jax.ShapeDtypeStruct(kept.shape[1:], jnp.float32)
    return order.call(kernel, (kept, arrived), (shape, shape))


def finished(order, stays, arrived, prior, scale):
    def kernel(mine, theirs, before, out):
        out[...] = before[...] + scale * (mine[...] + theirs[...])

    return order.call(
        kernel, (stays, arrived, prior), jax.ShapeDtypeStruct(stays.shape, jnp.float32)
    )


def assembled(order, near, far):
    half = near.shape[0]

    def kernel(here, away, out):
        place = lax.select(lax.axis_index("owner") < 2, 0, half)
        out[pl.ds(pl.multiple_of(place, half), half), :] = here[...]
        out[pl.ds(pl.multiple_of(half - place, half), half), :] = away[...]

    shape = jax.ShapeDtypeStruct((2 * half, near.shape[1]), near.dtype)
    return order.call(kernel, (near, far), shape)


def core_parts(order, bases, omegas):
    rank = omegas[0].shape[1]
    share = rank // lax.axis_size("context")
    count = len(bases)

    def kernel(*refs):
        out, product = refs[-2:]
        start = pl.multiple_of(lax.axis_index("context") * share, share)
        for k in range(count):
            product[...] = token_contract(refs[k][...], refs[count + k][...])
            out[k * share : (k + 1) * share, :] = product[pl.ds(start, share), :]

    shape = jax.ShapeDtypeStruct((count * share, rank), jnp.float32)
    scratch = [pltpu.VMEM((rank, rank), jnp.float32)]
    return order.call(kernel, (*bases, *omegas), shape, vmem=44 * MIB, scratch_shapes=scratch)


def lines_of_four(inputs, omegas, bases, eigens, scale):
    place = lax.axis_index("owner")
    inner = (place == 1) | (place == 2)
    turned = [x.shape[1] % 128 != 0 for x in inputs]
    inputs = [x.T if t else x for x, t in zip(inputs, turned)]
    order = Order()
    jobs = [(k, c) for k in (2, 0, 1) for c in range(CHUNKS)]
    count = len(jobs)
    partial, inward, pair, across, near, far, probe, outward = ([None] * count for _ in range(8))
    state = [None] * 3
    results = [None] * 3

    def multiply(i):
        k, c = jobs[i]
        rows = inputs[k].shape[1 if turned[k] else 0] // CHUNKS
        partial[i] = probe_rows(order, inputs[k], omegas[k], c * rows, rows, turned[k])
        if i == CARRIER:
            half, part = rows // 2, cores.shape[0] // 2
            pieces = [partial[i][:half], cores[:part], partial[i][half:], cores[part:]]
            partial[i] = jnp.concatenate(pieces, 0)
        inward[i] = lax.ppermute(partial[i], "owner", INWARD)

    def add_pair(i, after=()):
        kept, given = paired(order, partial[i], inward[i], after)
        pair[i] = kept
        across[i] = lax.ppermute(given, "owner", ACROSS)

    def add_across(i):
        exact = cores.shape[0] // 2 if i == CARRIER else 0
        near[i] = rounded(order, pair[i], across[i], exact)
        far[i] = lax.ppermute(near[i], "owner", ACROSS)

    def assemble(i):
        probe[i] = assembled(order, near[i], far[i])
        outward[i] = lax.ppermute(probe[i], "owner", OUTWARD)

    def carried(i):
        whole = lax.select(inner, probe[i], outward[i])
        if i != CARRIER:
            return whole, None
        part = cores.shape[0] // 2
        half = whole.shape[0] // 2
        plain = half - 3 * part
        terms = [
            whole[h * half + plain :][: 3 * part].reshape(3, part, -1).astype(jnp.float32)
            for h in range(2)
        ]
        total = jnp.concatenate([t[0] + (t[1] + t[2]) for t in terms], 0)
        return jnp.concatenate([whole[:plain], whole[half : half + plain]], 0), total

    def contract(k):
        pieces = [chunk[i] for i in range(count) if jobs[i][0] == k]
        data = data_rows(order, inputs[k], jnp.concatenate(pieces, 0), turned[k])
        if turned[k]:
            state[k] = lax.psum_scatter(data, "context", scatter_dimension=0, tiled=True)
        else:
            core = lax.axis_index("context") % 2
            state[k] = halves(data, core), lax.ppermute(halves(data, 1 - core), "context", PAIRED)

    def add_cores(k):
        stays, given = core_summed(order, *state[k])
        state[k] = stays, lax.ppermute(given, "context", SKIPPED)

    def finish(k):
        results[k] = finished(order, *state[k], priors[k], scale)

    rank = omegas[0].shape[1]
    chunk = [None] * count
    multiply(0)
    multiply(1)
    cores = core_parts(order, bases, omegas)
    priors = ()
    for i in range(count):
        after = () if i < 2 else (outward[i - 2],)
        add_pair(i, (*after, *priors) if i == CARRIER + 3 else after)
        if i + 2 < count:
            multiply(i + 2)
        if i > 1:
            chunk[i - 2], total = carried(i - 2)
            if i - 2 == CARRIER:
                total = lax.all_gather(total, "context", axis=0).reshape(4, 3, rank // 4, rank)
                total = [total[:, k].reshape(rank, rank) for k in range(3)]
                priors = [prior_rows(b, e, c) for b, e, c in zip(bases, eigens, total)]
        if i > 0:
            assemble(i - 1)
        if i > 1 and jobs[i - 2][1] == CHUNKS - 1:
            contract(jobs[i - 2][0])
        add_across(i)
    add_cores(0)
    assemble(count - 1)
    chunk[-2:] = [carried(i)[0] for i in (count - 2, count - 1)]
    contract(1)
    add_cores(1)
    finish(0)
    results[2] = priors[2] + scale * state[2]
    finish(1)
    return tuple(results)


def any_lines(inputs, omegas, bases, eigens, scale):
    cores = core_total(bases, omegas)
    results = []
    for x, w, b, e, core in zip(inputs, omegas, bases, eigens, cores):
        partial = jnp.dot(x, w, preferred_element_type=jnp.float32)
        share = lax.psum_scatter(partial, "owner", scatter_dimension=0, tiled=True)
        probe = lax.all_gather(share.astype(jnp.bfloat16), "owner", axis=0, tiled=True)
        data = lax.psum_scatter(
            token_contract(x, probe), "context", scatter_dimension=0, tiled=True
        )
        results.append(prior_rows(b, e, core) + scale * data)
    return tuple(results)


def per_device(
    x_attn,
    x_mlp,
    x_down,
    omega_attn,
    omega_mlp,
    omega_down,
    basis_attn,
    basis_mlp,
    basis_down,
    eig_attn,
    eig_mlp,
    eig_down,
):
    inputs = (x_attn, x_mlp, x_down)
    omegas = (omega_attn, omega_mlp, omega_down)
    bases = (basis_attn, basis_mlp, basis_down)
    eigens = (eig_attn, eig_mlp, eig_down)
    scale = 0.1 / (x_attn.shape[0] * lax.axis_size("context"))
    fours = lax.axis_size("owner") == 4 and lax.axis_size("context") == 4
    run = lines_of_four if fours else any_lines
    return run(inputs, omegas, bases, eigens, scale)


def solution(mesh):
    placed = (
        P(("section", "context"), "owner"),
        P(("section", "context"), "owner"),
        P(("section", "context"), "owner"),
        P(("section", "owner"), None),
        P(("section", "owner"), None),
        P(("section", "owner"), None),
        P(("section", "owner"), None),
        P(("section", "owner"), None),
        P(("section", "owner"), None),
        P("section"),
        P("section"),
        P("section"),
    )
    return jax.shard_map(
        per_device,
        mesh=mesh,
        in_specs=placed,
        out_specs=(
            P(("section", "owner", "context"), None),
            P(("section", "owner", "context"), None),
            P(("section", "owner", "context"), None),
        ),
        check_vma=False,
    )
```

time: 429 us -> 302 us (0.70)
  blocking collectives: 225 us -> 13.3 us
  matrix products: 79.8 us -> 4.87 us
  Pallas kernels: 0 us -> 65.6 us
  starting transfers between devices: 0.39 us -> 64.7 us
  local copies, waits for them, and re-layouts: 1.21 us -> 14.3 us
  waiting for transfers between devices: 106 us -> 116 us
  other arithmetic: 0 us -> 7.21 us
    psum x1 -> x0, blocking collectives: 225 us -> none  [per_device(): lax.psum((probes_local[0], probes_local[1], probes_local[2], cores_local[...]
    ppermute x0 -> x28, waiting for transfers between devices: none -> 116 us  [the longest x6 52.4 us: assemble(): outward[i] = lax.ppermute(probe[i], 'owner', OUTWARD)]
    reduce_scatter x3 -> x1, waiting for transfers between devices: 106 us -> 0.01 us  [contract(): lax.psum_scatter(data, 'context', scatter_dimension=0, tiled=True)]
    dot_general x9 -> x0, matrix products: 70.6 us -> none  [the longest x6 42 us: token_contract(): lax.dot_general(inputs, probe, (((0,), (0,)), ((), ())), preferred_elemen...]
    pallas_call x0 -> x32, Pallas kernels: none -> 65.6 us  [call(): pl.pallas_call(body, out_shape=out, in_specs=[*specs, *[ANYWHERE] * len(h...]
    ppermute x0 -> x28, starting transfers between devices: none -> 64.7 us  [the longest x6 44.6 us: multiply(): inward[i] = lax.ppermute(partial[i], 'owner', INWARD)]
    all_gather x0 -> x1, blocking collectives: none -> 13.3 us  [lines_of_four(): lax.all_gather(total, 'context', axis=0).reshape(4, 3, rank // 4, rank)]
    unnamed x18 -> x48, local copies, waits for them, and re-layouts: 1.21 us -> 13.8 us
  transfers between devices with their start and end apart: 4 -> 29, of which waited for: 3 -> 10; matrix products, arithmetic and copies ran while one was open for 16% -> 3% of each run, Pallas kernels for 0% -> 15%
where the time goes in v1:
time: 302 us; the launch traced here: 300 us
  waiting for transfers between devices  116 us (38%)
  Pallas kernels  65.6 us (22%)
  starting transfers between devices  64.7 us (21%)
  between operations  14.9 us (5%)
  local copies, waits for them, and re-layouts  14.3 us (5%)
  blocking collectives  13.3 us (4%)
  other arithmetic  7.21 us (2%)
  matrix products  4.87 us (2%)
    pallas_call x32, Pallas kernels, call(): pl.pallas_call(body, out_shape=out, in_specs=[*specs, *[ANYWHERE] * len(h...  65.6 us
    ppermute x6, waiting for transfers between devices, assemble(): outward[i] = lax.ppermute(probe[i], 'owner', OUTWARD)  52.4 us
    ppermute x6, starting transfers between devices, multiply(): inward[i] = lax.ppermute(partial[i], 'owner', INWARD)  44.6 us
    ppermute x6, waiting for transfers between devices, multiply(): inward[i] = lax.ppermute(partial[i], 'owner', INWARD)  41.1 us
    ppermute x2, waiting for transfers between devices, add_cores(): state[k] = (stays, lax.ppermute(given, 'context', SKIPPED))  20.7 us
    unnamed x48, local copies, waits for them, and re-layouts  13.8 us
    all_gather x1, blocking collectives, lines_of_four(): lax.all_gather(total, 'context', axis=0).reshape(4, 3, rank // 4, rank)  13.3 us
    ppermute x6, starting transfers between devices, assemble(): outward[i] = lax.ppermute(probe[i], 'owner', OUTWARD)  7.73 us
  transfers between devices with their start and end apart: 29, of which 10 were waited for; matrix products, arithmetic and copies ran while one was open for 3% of the time, Pallas kernels for 15%

profile of v1, /device:TPU:0, one launch (start us, length us, event | category | flops | bytes accessed | tf_op | source)
XLA Modules:
  0.0 300.4 jit_solution(18090729369101683080)
XLA Ops:
  9.3 7.5 %shard_map.139.refs_2_.refs_0_ = f32[1024,256]{1,0:T(8,128)S(1)} custom-call(bf16[7392,2048]{1,0:T(8,128)(2,1)} %bitcast.31, bf16[7392,256]{1,0:T(8,128)(2,1)S(1)} %copy-done.2), custom_call_target="tpu_custom_call" | custom-call | flops 1000 | bytes 1000 | tf_op jit(solution)/shard_map/pallas_call | solution.py:60
  16.9 5.3 %collective-permute-start = (f32[1024,256]{1,0:T(8,128)S(1)}, f32[1024,256]{1,0:T(8,128)S(1)}, u32[]{:S(2)}, u32[]{:S(2)}) collective-permute-start(f32[1024,256]{1,0:T(8,128)S(1)} %shard_map.139.refs_2_.refs_0_), channel_id=1, source_target_pairs={{0,4},{12,8},{1,5},{13,9},{2,6},{14,10},{3,7},{15,11},{16,20},{28,... | collective-permute-start | bytes 3145736 | tf_op jit(solution)/shard_map/ppermute | solution.py:230
  22.1 7.7 %shard_map.140.refs_6_.refs_0_ = f32[1024,256]{1,0:T(8,128)S(1)} custom-call(bf16[7392,2048]{1,0:T(8,128)(2,1)} %bitcast.32, bf16[7392,256]{1,0:T(8,128)(2,1)S(1)} %copy-done.2, f32[1024,256]{1,0:T(8,128)S(1)} %shard_map.139.refs_2_.refs_0_), custom_call_target="tpu_custom_call" | custom-call | flops 1000 | bytes 1000 | tf_op jit(solution)/shard_map/pallas_call | solution.py:60
  31.3 3.9 %shard_map.141.refs_2_ = f32[192,256]{1,0:T(8,128)S(1)} custom-call(bf16[2048,256]{1,0:T(8,128)(2,1)S(1)} %copy-done.10, bf16[2048,256]{1,0:T(8,128)(2,1)S(1)} %copy-done.11, bf16[7392,256]{1,0:T(8,128)(2,1)S(1)} %copy-done.5, bf16[2048,256]{1,0:T(8,128)(2,1)S(1)} %copy-done.3, bf16[2048,256]{1,0:T(8,128)(2,1)S(1)} %copy-done.4, bf16[7392,256]{1,0:T(8,128)(2,1)} %refs_5_.1, ...), custom_call_target="tpu_custom_call" | custom-call | flops 1000 | bytes 1000 | tf_op jit(solution)/shard_map/pallas_call | solution.py:60
  35.2 10.4 %collective-permute-done.refs_1_ = f32[1024,256]{1,0:T(8,128)S(1)} collective-permute-done((f32[1024,256]{1,0:T(8,128)S(1)}, f32[1024,256]{1,0:T(8,128)S(1)}, u32[]{:S(2)}, u32[]{:S(2)}) %collective-permute-start) | collective-permute-done | bytes 1048608 | tf_op jit(solution)/shard_map/ppermute | solution.py:230
  46.4 3.1 %shard_map.143.refs_2_ = f32[1024,256]{1,0:T(8,128)S(1)} custom-call(bf16[2048,2048]{1,0:T(8,128)(2,1)} %refs_0_.12, bf16[2048,256]{1,0:T(8,128)(2,1)S(1)} %copy-done.3, f32[512,256]{1,0:T(8,128)S(1)} %get-tuple-element.19.refs_2_), custom_call_target="tpu_custom_call" | custom-call | flops 1000 | bytes 1000 | tf_op jit(solution)/shard_map/pallas_call | solution.py:60
  49.7 7.3 %collective-permute-start.1 = (f32[1216,256]{1,0:T(8,128)S(1)}, f32[1216,256]{1,0:T(8,128)S(1)}, u32[]{:S(2)}, u32[]{:S(2)}) collective-permute-start(f32[1216,256]{1,0:T(8,128)S(1)} %pad_maximum_fusion.refs_0_), channel_id=1, source_target_pairs={{0,4},{12,8},{1,5},{13,9},{2,6},{14,10},{3,7},{15,11},{16,20},{28,... | collective-permute-start | bytes 3735560 | tf_op jit(solution)/shard_map/ppermute | solution.py:230
  57.7 10.4 %collective-permute-done.2.refs_1_ = f32[1024,256]{1,0:T(8,128)S(1)} collective-permute-done((f32[1024,256]{1,0:T(8,128)S(1)}, f32[1024,256]{1,0:T(8,128)S(1)}, u32[]{:S(2)}, u32[]{:S(2)}) %collective-permute-start.2) | collective-permute-done | bytes 1048608 | tf_op jit(solution)/shard_map/ppermute | solution.py:230
  68.9 3.1 %shard_map.146.refs_2_.refs_0_ = f32[1024,256]{1,0:T(8,128)S(1)} custom-call(bf16[2048,2048]{1,0:T(8,128)(2,1)} %refs_0_.12, bf16[2048,256]{1,0:T(8,128)(2,1)S(1)} %copy-done.3, f32[512,256]{1,0:T(8,128)S(1)} %get-tuple-element.22.refs_2_), custom_call_target="tpu_custom_call" | custom-call | flops 1000 | bytes 1000 | tf_op jit(solution)/shard_map/pallas_call | solution.py:60
  74.1 19.5 %collective-permute-done.1.refs_1_ = f32[1216,256]{1,0:T(8,128)S(1)} collective-permute-done((f32[1216,256]{1,0:T(8,128)S(1)}, f32[1216,256]{1,0:T(8,128)S(1)}, u32[]{:S(2)}, u32[]{:S(2)}) %collective-permute-start.1) | collective-permute-done | bytes 1245216 | tf_op jit(solution)/shard_map/ppermute | solution.py:230
  96.1 7.4 %collective-permute-start.10 = (f32[1024,256]{1,0:T(8,128)S(1)}, f32[1024,256]{1,0:T(8,128)}, u32[]{:S(2)}, u32[]{:S(2)}) collective-permute-start(f32[1024,256]{1,0:T(8,128)S(1)} %shard_map.146.refs_2_.refs_0_), channel_id=1, source_target_pairs={{0,4},{12,8},{1,5},{13,9},{2,6},{14,10},{3,7},{15,11},{16,20},{28,... | collective-permute-start | bytes 3145736 | tf_op jit(solution)/shard_map/ppermute | solution.py:230
  113.0 8.9 %collective-permute-done.11.refs_3_ = bf16[1024,256]{1,0:T(8,128)(2,1)} collective-permute-done((bf16[1024,256]{1,0:T(8,128)(2,1)}, bf16[1024,256]{1,0:T(8,128)(2,1)}, u32[]{:S(2)}, u32[]{:S(2)}) %collective-permute-start.11) | collective-permute-done | bytes 524320 | tf_op jit(solution)/shard_map/ppermute | solution.py:244
  125.1 4.2 %shard_map.154.refs_2_.refs_0_ = f32[1024,256]{1,0:T(8,128)} custom-call(bf16[2048,2048]{1,0:T(8,128)(2,1)} %refs_0_.13, bf16[2048,256]{1,0:T(8,128)(2,1)S(1)} %copy-done.4, f32[512,256]{1,0:T(8,128)S(1)} %get-tuple-element.25.refs_2_), custom_call_target="tpu_custom_call" | custom-call | flops 1000 | bytes 1000 | tf_op jit(solution)/shard_map/pallas_call | solution.py:60
  129.4 13.5 %shard_map.156.refs_2_ = f32[7392,256]{1,0:T(8,128)S(1)} custom-call(bf16[7392,2048]{1,0:T(8,128)(2,1)} %bitcast.33, bf16[2048,256]{1,0:T(8,128)(2,1)S(1)} %pad_maximum_fusion.1.refs_1_, bf16[1600,256]{1,0:T(8,128)(2,1)S(1)} %shard_map.155.refs_2_), custom_call_target="tpu_custom_call" | custom-call | flops 1000 | bytes 1000 | tf_op jit(solution)/shard_map/pallas_call | solution.py:60
  145.9 5.6 %collective-permute-start.15 = (f32[1024,256]{1,0:T(8,128)S(1)}, f32[1024,256]{1,0:T(8,128)}, u32[]{:S(2)}, u32[]{:S(2)}) collective-permute-start(f32[1024,256]{1,0:T(8,128)S(1)} %shard_map.150.refs_2_.refs_0_), channel_id=1, source_target_pairs={{0,4},{12,8},{1,5},{13,9},{2,6},{14,10},{3,7},{15,11},{16,20},{28,... | collective-permute-start | bytes 3145736 | tf_op jit(solution)/shard_map/ppermute | solution.py:230
  153.5 4.8 %copy-done.1 = f32[7392,256]{1,0:T(8,128)S(1)} copy-done((f32[7392,256]{1,0:T(8,128)S(1)}, f32[7392,256]{1,0:T(8,128)}, u32[]{:S(2)}) %copy-start.1) | copy-done | bytes 7569432
  159.0 17.8 %collective-permute-start.19 = (f32[1024,256]{1,0:T(8,128)}, f32[1024,256]{1,0:T(8,128)S(1)}, u32[]{:S(2)}, u32[]{:S(2)}) collective-permute-start(f32[1024,256]{1,0:T(8,128)} %shard_map.154.refs_2_.refs_0_), channel_id=1, source_target_pairs={{0,4},{12,8},{1,5},{13,9},{2,6},{14,10},{3,7},{15,11},{16,20},{28,... | collective-permute-start | bytes 3145736 | tf_op jit(solution)/shard_map/ppermute | solution.py:230
  180.5 13.3 %all-gather = f32[768,256]{1,0:T(8,128)S(1)} all-gather(f32[192,256]{1,0:T(8,128)S(1)} %pad_maximum_fusion.4), channel_id=2, replica_groups=mesh['section'=2,'owner'=4,'context'=4] {'context'}, dimensions={0}, use_global_device_ids=true | all-gather | bytes 983040 | tf_op jit(solution)/shard_map/all_gather | solution.py:290
  203.9 4.9 %shard_map.163.refs_2_ = f32[2048,256]{1,0:T(8,128)S(1)} custom-call(bf16[2048,2048]{1,0:T(8,128)(2,1)} %refs_0_.12, bf16[2048,256]{1,0:T(8,128)(2,1)S(1)} %copy-done.7, bf16[1024,256]{1,0:T(8,128)(2,1)S(1)} %shard_map.162.refs_2_), custom_call_target="tpu_custom_call" | custom-call | flops 1000 | bytes 1000 | tf_op jit(solution)/shard_map/pallas_call | solution.py:60
  214.1 23.0 %collective-permute-done.23 = bf16[1024,256]{1,0:T(8,128)(2,1)S(1)} collective-permute-done((bf16[1024,256]{1,0:T(8,128)(2,1)S(1)}, bf16[1024,256]{1,0:T(8,128)(2,1)S(1)}, u32[]{:S(2)}, u32[]{:S(2)}) %collective-permute-start.23) | collective-permute-done | bytes 524320 | tf_op jit(solution)/shard_map/ppermute | solution.py:244
  237.2 20.5 %collective-permute-done.25 = bf16[1024,256]{1,0:T(8,128)(2,1)S(1)} collective-permute-done((bf16[1024,256]{1,0:T(8,128)(2,1)S(1)}, bf16[1024,256]{1,0:T(8,128)(2,1)S(1)}, u32[]{:S(2)}, u32[]{:S(2)}) %collective-permute-start.25) | collective-permute-done | bytes 524320 | tf_op jit(solution)/shard_map/ppermute | solution.py:244
  257.8 4.9 %shard_map.167.refs_2_ = f32[2048,256]{1,0:T(8,128)S(1)} custom-call(bf16[2048,2048]{1,0:T(8,128)(2,1)} %refs_0_.13, bf16[2048,256]{1,0:T(8,128)(2,1)S(1)} %pad_maximum_fusion.3.refs_1_, bf16[1024,256]{1,0:T(8,128)(2,1)S(1)} %shard_map.166.refs_2_), custom_call_target="tpu_custom_call" | custom-call | flops 1000 | bytes 1000 | tf_op jit(solution)/shard_map/pallas_call | solution.py:60
  267.0 10.8 %collective-permute-done.22.refs_1_ = f32[512,256]{1,0:T(8,128)S(1)} collective-permute-done((f32[512,256]{1,0:T(8,128)S(1)}, f32[512,256]{1,0:T(8,128)S(1)}, u32[]{:S(2)}, u32[]{:S(2)}) %collective-permute-start.22) | collective-permute-done | bytes 524320 | tf_op jit(solution)/shard_map/ppermute | solution.py:271
  278.7 9.9 %collective-permute-done.27.refs_1_ = f32[512,256]{1,0:T(8,128)S(1)} collective-permute-done((f32[512,256]{1,0:T(8,128)S(1)}, f32[512,256]{1,0:T(8,128)S(1)}, u32[]{:S(2)}, u32[]{:S(2)}) %collective-permute-start.27) | collective-permute-done | bytes 524320 | tf_op jit(solution)/shard_map/ppermute | solution.py:271
  (142 shorter events, 57.9 us)
Async XLA Ops:
  7.2 283.4 %reduce-scatter.2.cloned.1.call-start = ((), (), s32[]{:S(2)}) async-start(), calls=%async_computation.1 | async-start | bytes 9461760 | tf_op jit(solution)/shard_map/reduce_scatter | solution.py:264
  16.9 28.7 %collective-permute-start = (f32[1024,256]{1,0:T(8,128)S(1)}, f32[1024,256]{1,0:T(8,128)S(1)}, u32[]{:S(2)}, u32[]{:S(2)}) collective-permute-start(f32[1024,256]{1,0:T(8,128)S(1)} %shard_map.139.refs_2_.refs_0_), channel_id=1, source_target_pairs={{0,4},{12,8},{1,5},{13,9},{2,6},{14,10},{3,7},{15,11},{16,20},{28,... | collective-permute-start | bytes 3145736 | tf_op jit(solution)/shard_map/ppermute | solution.py:230
  29.8 38.2 %collective-permute-start.2 = (f32[1024,256]{1,0:T(8,128)S(1)}, f32[1024,256]{1,0:T(8,128)S(1)}, u32[]{:S(2)}, u32[]{:S(2)}) collective-permute-start(f32[1024,256]{1,0:T(8,128)S(1)} %shard_map.140.refs_6_.refs_0_), channel_id=1, source_target_pairs={{0,4},{12,8},{1,5},{13,9},{2,6},{14,10},{3,7},{15,11},{16,20},{28,... | collective-permute-start | bytes 3145736 | tf_op jit(solution)/shard_map/ppermute | solution.py:230
  45.7 11.2 %collective-permute-start.3 = (f32[512,256]{1,0:T(8,128)S(1)}, f32[512,256]{1,0:T(8,128)S(1)}, u32[]{:S(2)}, u32[]{:S(2)}) collective-permute-start(f32[512,256]{1,0:T(8,128)S(1)} %get-tuple-element.19.refs_2_), channel_id=1, source_target_pairs={{4,8},{8,4},{5,9},{9,5},{6,10},{10,6},{7,11},{11,7},{20,24},{24,20... | collective-permute-start | bytes 1572872 | tf_op jit(solution)/shard_map/ppermute | solution.py:235
  49.7 44.0 %collective-permute-start.1 = (f32[1216,256]{1,0:T(8,128)S(1)}, f32[1216,256]{1,0:T(8,128)S(1)}, u32[]{:S(2)}, u32[]{:S(2)}) collective-permute-start(f32[1216,256]{1,0:T(8,128)S(1)} %pad_maximum_fusion.refs_0_), channel_id=1, source_target_pairs={{0,4},{12,8},{1,5},{13,9},{2,6},{14,10},{3,7},{15,11},{16,20},{28,... | collective-permute-start | bytes 3735560 | tf_op jit(solution)/shard_map/ppermute | solution.py:230
  57.0 15.0 %collective-permute-start.5 = (bf16[512,256]{1,0:T(8,128)(2,1)S(1)}, bf16[512,256]{1,0:T(8,128)(2,1)S(1)}, u32[]{:S(2)}, u32[]{:S(2)}) collective-permute-start(bf16[512,256]{1,0:T(8,128)(2,1)S(1)} %shard_map.144.refs_2_.refs_0_), channel_id=1, source_target_pairs={{4,8},{8,4},{5,9},{9,5},{6,10},{10,6},{7,11},{11,7},{20,24},{24,20... | collective-permute-start | bytes 786440 | tf_op jit(solution)/shard_map/ppermute | solution.py:240
  68.2 5.1 %collective-permute-start.4 = (f32[512,256]{1,0:T(8,128)S(1)}, f32[512,256]{1,0:T(8,128)S(1)}, u32[]{:S(2)}, u32[]{:S(2)}) collective-permute-start(f32[512,256]{1,0:T(8,128)S(1)} %get-tuple-element.22.refs_2_), channel_id=1, source_target_pairs={{4,8},{8,4},{5,9},{9,5},{6,10},{10,6},{7,11},{11,7},{20,24},{24,20... | collective-permute-start | bytes 1572872 | tf_op jit(solution)/shard_map/ppermute | solution.py:235
  72.0 21.6 %collective-permute-start.6 = (bf16[1024,256]{1,0:T(8,128)(2,1)S(1)}, bf16[1024,256]{1,0:T(8,128)(2,1)S(1)}, u32[]{:S(2)}, u32[]{:S(2)}) collective-permute-start(bf16[1024,256]{1,0:T(8,128)(2,1)S(1)} %shard_map.147.refs_2_), channel_id=1, source_target_pairs={{4,0},{8,12},{5,1},{9,13},{6,2},{10,14},{7,3},{11,15},{20,16},{24,... | collective-permute-start | bytes 1572872 | tf_op jit(solution)/shard_map/ppermute | solution.py:244
  73.4 33.2 %collective-permute-start.8 = (bf16[512,256]{1,0:T(8,128)(2,1)S(1)}, bf16[512,256]{1,0:T(8,128)(2,1)S(1)}, u32[]{:S(2)}, u32[]{:S(2)}) collective-permute-start(bf16[512,256]{1,0:T(8,128)(2,1)S(1)} %shard_map.148.refs_2_.refs_0_), channel_id=1, source_target_pairs={{4,8},{8,4},{5,9},{9,5},{6,10},{10,6},{7,11},{11,7},{20,24},{24,20... | collective-permute-start | bytes 786440 | tf_op jit(solution)/shard_map/ppermute | solution.py:240
  94.6 15.2 %collective-permute-start.7 = (f32[608,256]{1,0:T(8,128)}, f32[608,256]{1,0:T(8,128)}, u32[]{:S(2)}, u32[]{:S(2)}) collective-permute-start(f32[608,256]{1,0:T(8,128)} %get-tuple-element.24.refs_2_), channel_id=1, source_target_pairs={{4,8},{8,4},{5,9},{9,5},{6,10},{10,6},{7,11},{11,7},{20,24},{24,20... | collective-permute-start | bytes 1867784 | tf_op jit(solution)/shard_map/ppermute | solution.py:235
  96.1 27.6 %collective-permute-start.10 = (f32[1024,256]{1,0:T(8,128)S(1)}, f32[1024,256]{1,0:T(8,128)}, u32[]{:S(2)}, u32[]{:S(2)}) collective-permute-start(f32[1024,256]{1,0:T(8,128)S(1)} %shard_map.146.refs_2_.refs_0_), channel_id=1, source_target_pairs={{0,4},{12,8},{1,5},{13,9},{2,6},{14,10},{3,7},{15,11},{16,20},{28,... | collective-permute-start | bytes 3145736 | tf_op jit(solution)/shard_map/ppermute | solution.py:230
  107.4 14.4 %collective-permute-start.11 = (bf16[1024,256]{1,0:T(8,128)(2,1)}, bf16[1024,256]{1,0:T(8,128)(2,1)}, u32[]{:S(2)}, u32[]{:S(2)}) collective-permute-start(bf16[1024,256]{1,0:T(8,128)(2,1)} %shard_map.151.refs_2_), channel_id=1, source_target_pairs={{4,0},{8,12},{5,1},{9,13},{6,2},{10,14},{7,3},{11,15},{20,16},{24,... | collective-permute-start | bytes 1572872 | tf_op jit(solution)/shard_map/ppermute | solution.py:244
  112.1 17.2 %collective-permute-start.9 = (bf16[800,256]{1,0:T(8,128)(2,1)S(1)}, bf16[800,256]{1,0:T(8,128)(2,1)S(1)}, u32[]{:S(2)}, u32[]{:S(2)}) collective-permute-start(bf16[800,256]{1,0:T(8,128)(2,1)S(1)} %shard_map.152.refs_2_.refs_0_), channel_id=1, source_target_pairs={{4,8},{8,4},{5,9},{9,5},{6,10},{10,6},{7,11},{11,7},{20,24},{24,20... | collective-permute-start | bytes 1228808 | tf_op jit(solution)/shard_map/ppermute | solution.py:240
  145.9 30.9 %collective-permute-start.15 = (f32[1024,256]{1,0:T(8,128)S(1)}, f32[1024,256]{1,0:T(8,128)}, u32[]{:S(2)}, u32[]{:S(2)}) collective-permute-start(f32[1024,256]{1,0:T(8,128)S(1)} %shard_map.150.refs_2_.refs_0_), channel_id=1, source_target_pairs={{0,4},{12,8},{1,5},{13,9},{2,6},{14,10},{3,7},{15,11},{16,20},{28,... | collective-permute-start | bytes 3145736 | tf_op jit(solution)/shard_map/ppermute | solution.py:230
  151.5 25.3 %collective-permute-start.12 = (bf16[1600,256]{1,0:T(8,128)(2,1)S(1)}, bf16[1600,256]{1,0:T(8,128)(2,1)S(1)}, u32[]{:S(2)}, u32[]{:S(2)}) collective-permute-start(bf16[1600,256]{1,0:T(8,128)(2,1)S(1)} %shard_map.155.refs_2_), channel_id=1, source_target_pairs={{4,0},{8,12},{5,1},{9,13},{6,2},{10,14},{7,3},{11,15},{20,16},{24,... | collective-permute-start | bytes 2457608 | tf_op jit(solution)/shard_map/ppermute | solution.py:244
  158.3 20.6 %collective-permute-start.14 = (bf16[512,256]{1,0:T(8,128)(2,1)S(1)}, bf16[512,256]{1,0:T(8,128)(2,1)S(1)}, u32[]{:S(2)}, u32[]{:S(2)}) collective-permute-start(bf16[512,256]{1,0:T(8,128)(2,1)S(1)} %shard_map.157.refs_2_.refs_0_), channel_id=1, source_target_pairs={{4,8},{8,4},{5,9},{9,5},{6,10},{10,6},{7,11},{11,7},{20,24},{24,20... | collective-permute-start | bytes 786440 | tf_op jit(solution)/shard_map/ppermute | solution.py:240
  159.0 40.9 %collective-permute-start.19 = (f32[1024,256]{1,0:T(8,128)}, f32[1024,256]{1,0:T(8,128)S(1)}, u32[]{:S(2)}, u32[]{:S(2)}) collective-permute-start(f32[1024,256]{1,0:T(8,128)} %shard_map.154.refs_2_.refs_0_), channel_id=1, source_target_pairs={{0,4},{12,8},{1,5},{13,9},{2,6},{14,10},{3,7},{15,11},{16,20},{28,... | collective-permute-start | bytes 3145736 | tf_op jit(solution)/shard_map/ppermute | solution.py:230
  178.2 20.9 %collective-permute-start.17 = (f32[512,256]{1,0:T(8,128)S(1)}, f32[512,256]{1,0:T(8,128)S(1)}, u32[]{:S(2)}, u32[]{:S(2)}) collective-permute-start(f32[512,256]{1,0:T(8,128)S(1)} %get-tuple-element.27.refs_2_), channel_id=1, source_target_pairs={{4,8},{8,4},{5,9},{9,5},{6,10},{10,6},{7,11},{11,7},{20,24},{24,20... | collective-permute-start | bytes 1572872 | tf_op jit(solution)/shard_map/ppermute | solution.py:235
  178.9 20.9 %collective-permute-start.16 = (bf16[1024,256]{1,0:T(8,128)(2,1)S(1)}, bf16[1024,256]{1,0:T(8,128)(2,1)S(1)}, u32[]{:S(2)}, u32[]{:S(2)}) collective-permute-start(bf16[1024,256]{1,0:T(8,128)(2,1)S(1)} %shard_map.159.refs_2_), channel_id=1, source_target_pairs={{4,0},{8,12},{5,1},{9,13},{6,2},{10,14},{7,3},{11,15},{20,16},{24,... | collective-permute-start | bytes 1572872 | tf_op jit(solution)/shard_map/ppermute | solution.py:244
  209.0 3.6 %collective-permute-start.20 = (f32[2,512,256]{2,1,0:T(8,128)S(1)}, f32[2,512,256]{2,1,0:T(8,128)S(1)}, u32[]{:S(2)}, u32[]{:S(2)}) collective-permute-start(f32[2,512,256]{2,1,0:T(8,128)S(1)} %get-tuple-element.37), channel_id=1, source_target_pairs={{0,1},{1,0},{2,3},{3,2},{4,5},{5,4},{6,7},{7,6},{8,9},{9,8},{10,11... | collective-permute-start | bytes 3145736 | tf_op jit(solution)/shard_map/ppermute | solution.py:267
  210.5 26.5 %collective-permute-start.23 = (bf16[1024,256]{1,0:T(8,128)(2,1)S(1)}, bf16[1024,256]{1,0:T(8,128)(2,1)S(1)}, u32[]{:S(2)}, u32[]{:S(2)}) collective-permute-start(bf16[1024,256]{1,0:T(8,128)(2,1)S(1)} %shard_map.162.refs_2_), channel_id=1, source_target_pairs={{4,0},{8,12},{5,1},{9,13},{6,2},{10,14},{7,3},{11,15},{20,16},{24,... | collective-permute-start | bytes 1572872 | tf_op jit(solution)/shard_map/ppermute | solution.py:244
  212.8 44.9 %collective-permute-start.25 = (bf16[1024,256]{1,0:T(8,128)(2,1)S(1)}, bf16[1024,256]{1,0:T(8,128)(2,1)S(1)}, u32[]{:S(2)}, u32[]{:S(2)}) collective-permute-start(bf16[1024,256]{1,0:T(8,128)(2,1)S(1)} %shard_map.166.refs_2_), channel_id=1, source_target_pairs={{4,0},{8,12},{5,1},{9,13},{6,2},{10,14},{7,3},{11,15},{20,16},{24,... | collective-permute-start | bytes 1572872 | tf_op jit(solution)/shard_map/ppermute | solution.py:244
  263.0 14.8 %collective-permute-start.22 = (f32[512,256]{1,0:T(8,128)S(1)}, f32[512,256]{1,0:T(8,128)S(1)}, u32[]{:S(2)}, u32[]{:S(2)}) collective-permute-start(f32[512,256]{1,0:T(8,128)S(1)} %get-tuple-element.32.refs_2_), channel_id=1, source_target_pairs={{0,2},{2,0},{1,3},{3,1},{4,6},{6,4},{5,7},{7,5},{8,10},{10,8},{9,1... | collective-permute-start | bytes 1572872 | tf_op jit(solution)/shard_map/ppermute | solution.py:271
  265.8 22.8 %collective-permute-start.27 = (f32[512,256]{1,0:T(8,128)S(1)}, f32[512,256]{1,0:T(8,128)S(1)}, u32[]{:S(2)}, u32[]{:S(2)}) collective-permute-start(f32[512,256]{1,0:T(8,128)S(1)} %get-tuple-element.33.refs_3_), channel_id=1, source_target_pairs={{0,2},{2,0},{1,3},{3,1},{4,6},{6,4},{5,7},{7,5},{8,10},{10,8},{9,1... | collective-permute-start | bytes 1572872 | tf_op jit(solution)/shard_map/ppermute | solution.py:271
  (29 other events, 175.2 us)
Sparse Core Ops, SparseCore 0:
  146.0 71.4 reduce-scatter.1

commit v2 on v1

v2 whole, which is shorter than its diff:
```python
import math

import jax
import jax.numpy as jnp
from jax import lax
from jax.experimental import pallas as pl
from jax.experimental.pallas import tpu as pltpu
from jax.sharding import PartitionSpec as P

INWARD = ((0, 1), (3, 2))
ACROSS = ((1, 2), (2, 1))
OUTWARD = ((1, 0), (2, 3))
PAIRED = ((0, 1), (1, 0), (2, 3), (3, 2))
SKIPPED = ((0, 2), (2, 0), (1, 3), (3, 1))
CHUNKS = ((2, 8), (2, 8), (0, 8), (0, 8), (1, 8), (1, 8))
CARRIER = 2
FINE, COARSE = 65535.0, 32500.0
MIB = 1024 * 1024
FIRST = (((0,), (0,)), ((), ()))
ANYWHERE = pl.BlockSpec(memory_space=pl.ANY)


def token_contract(inputs, probe):
    return lax.dot_general(inputs, probe, FIRST, preferred_element_type=jnp.float32)


def prior_rows(basis, eigen, core):
    rows = basis.shape[0] // lax.axis_size("context")
    picked = lax.dynamic_slice_in_dim(basis, lax.axis_index("context") * rows, rows, 0)
    weighted = eigen[:, None] * core
    return 0.9 * jnp.dot(picked.astype(jnp.float32), weighted, precision=lax.Precision.HIGHEST)


def core_total(bases, omegas):
    size = lax.axis_size("context")
    rank = omegas[0].shape[1]
    share = rank // size
    start = lax.axis_index("context") * share
    mine = [
        token_contract(lax.dynamic_slice_in_dim(b, start, share, 1), w)
        for b, w in zip(bases, omegas)
    ]
    summed = lax.psum(jnp.concatenate(mine, 0), "owner")
    whole = lax.all_gather(summed, "context", axis=0)
    whole = whole.reshape(size, len(bases), share, rank)
    return [whole[:, k].reshape(rank, rank) for k in range(len(bases))]


class Order:
    def __init__(self):
        self.last = ()

    def call(self, kernel, operands, out, after=(), vmem=8 * MIB, **rest):
        held = (*self.last, *after)
        count = len(operands)
        outs = out if isinstance(out, tuple) else (out,)
        steps = len(rest.get("grid", ()))

        def body(*refs):
            results = refs[count + len(held) :]
            mark = results[len(outs)]
            mark[...] = jnp.zeros_like(mark)
            kernel(*refs[:count], *results[: len(outs)], *results[len(outs) + 1 :])

        whole = pl.BlockSpec(memory_space=pltpu.VMEM)
        specs = rest.pop("in_specs", [whole] * count)
        out_specs = rest.pop("out_specs", [whole] * len(outs))
        zeros = (0, 0)
        marked = pl.BlockSpec((8, 128), lambda *_: zeros) if steps else whole
        *result, mark = pl.pallas_call(
            body,
            out_shape=(*outs, jax.ShapeDtypeStruct((8, 128), jnp.float32)),
            in_specs=[*specs, *[ANYWHERE] * len(held)],
            out_specs=[*out_specs, marked],
            compiler_params=pltpu.CompilerParams(vmem_limit_bytes=vmem),
            **rest,
        )(*operands, *held)
        self.last = (mark,)
        return tuple(result) if isinstance(out, tuple) else result[0]

    def gate(self, array, after=(), hbm=False):
        return self.call(
            lambda *_: None,
            (array,),
            pltpu.HBM(array.shape, array.dtype) if hbm else jax.ShapeDtypeStruct(array.shape, array.dtype),
            after,
            MIB,
            in_specs=[pl.BlockSpec(memory_space=pltpu.HBM) if hbm else ANYWHERE],
            out_specs=[pl.BlockSpec(memory_space=pltpu.HBM) if hbm else ANYWHERE],
            input_output_aliases={0: 0},
        )


def probe_rows(order, inputs, omega, start, rows, turned):
    tile = math.gcd(512, start, rows)
    rank = omega.shape[1]
    first = start // tile

    def kernel(x, w, out):
        if turned:
            out[...] = token_contract(x[...], w[...])
        else:
            out[...] = jnp.dot(x[...], w[...], preferred_element_type=jnp.float32)

    depth = omega.shape[0]
    if turned:
        spec = pl.BlockSpec((depth, tile), lambda i: (0, first + i))
    else:
        spec = pl.BlockSpec((tile, depth), lambda i: (first + i, 0))
    return order.call(
        kernel,
        (inputs, omega),
        jax.ShapeDtypeStruct((rows, rank), jnp.float32),
        vmem=52 * MIB,
        grid=(rows // tile,),
        in_specs=[spec, pl.BlockSpec((depth, rank), lambda i: (0, 0))],
        out_specs=[pl.BlockSpec((tile, rank), lambda i: (i, 0))],
    )


def third(rows):
    return -(-rows // 24) * 8


def peaks(values):
    return jnp.maximum(jnp.max(jnp.abs(values), axis=1, keepdims=True), 1e-30)


def diagonal(rows, rank):
    shape = (rows, rank)
    return lax.broadcasted_iota(jnp.int32, shape, 0) == lax.broadcasted_iota(jnp.int32, shape, 1)


def pack(value, out, plain):
    group = third(plain)
    left = plain - 2 * group
    rank = value.shape[1]
    peak = peaks(value[:plain, :])
    scale = FINE / peak
    first = jnp.round(value[:group, :] * scale[:group])
    second = jnp.round(value[group : 2 * group, :] * scale[group : 2 * group])
    last = jnp.round(value[2 * group : plain, :] * (COARSE / peak[2 * group :]))
    high = jnp.round(last * (1 / 255))
    low = last - high * 255
    first, second = first * 256, second * 256
    out[:left, :] = first[:left] + high
    out[group : group + left, :] = second[:left] + low
    if left < group:
        out[left:group, :] = first[left:]
        out[group + left : 2 * group, :] = second[left:]
    out[2 * group : 2 * group + 8, :] = jnp.zeros((8, rank), jnp.float32)
    for k, start in enumerate(range(0, plain, rank)):
        part = peak[start : start + rank]
        row = jnp.where(diagonal(part.shape[0], rank), part, 0.0)
        out[2 * group + k : 2 * group + k + 1, :] = jnp.sum(row, axis=0, keepdims=True)
    if value.shape[0] > plain:
        out[2 * group + 8 :, :] = value[plain:, :]


def add_packed(mine, packed, plain):
    group = third(plain)
    left = plain - 2 * group
    rank = mine.shape[1]
    pieces = []
    for k, start in enumerate(range(0, plain, rank)):
        mask = diagonal(min(rank, plain - start), rank)
        row = jnp.where(mask, packed[2 * group + k : 2 * group + k + 1, :], 0.0)
        pieces.append(jnp.sum(row, axis=1, keepdims=True))
    peak = jnp.concatenate(pieces, 0)
    unit = peak * (1 / FINE)
    first, second = packed[:group, :], packed[group : 2 * group, :]
    whole = jnp.round(first * (1 / 256))
    high = first - whole * 256
    other = jnp.round(second * (1 / 256))
    low = second - other * 256
    last = high[:left] * 255 + low[:left]
    return (
        (0, group, mine[:group, :] + whole * unit[:group]),
        (group, 2 * group, mine[group : 2 * group, :] + other * unit[group : 2 * group]),
        (2 * group, plain, mine[2 * group : plain, :] + last * (peak[2 * group :] * (1 / COARSE))),
    )


def packed_shape(value, plain):
    rows = 2 * third(plain) + 8 + value.shape[0] - plain
    return jax.ShapeDtypeStruct((rows, value.shape[1]), jnp.float32)


def packed(order, partial, plain):
    return order.call(
        lambda value, out: pack(value, out, plain), (partial,), packed_shape(partial, plain)
    )


def paired(order, partial, arrived, plain):
    def kernel(mine, theirs, out, message):
        for start, stop, rows in add_packed(mine, theirs, plain):
            out[start:stop, :] = rows
        if mine.shape[0] > plain:
            out[plain:, :] = mine[plain:, :] + theirs[2 * third(plain) + 8 :, :]
        pack(out, message, plain)

    shape = jax.ShapeDtypeStruct(partial.shape, jnp.float32)
    return order.call(kernel, (partial, arrived), (shape, packed_shape(partial, plain)))


def rounded(order, pair, arrived, plain):
    rows, rank = pair.shape
    exact = rows - plain

    def kernel(mine, theirs, out):
        for start, stop, total in add_packed(mine, theirs, plain):
            out[start:stop, :] = total.astype(jnp.bfloat16)
        if exact:
            rest = mine[plain:, :] + theirs[2 * third(plain) + 8 :, :]
            for i in range(3):
                term = rest.astype(jnp.bfloat16)
                out[plain + i * exact : plain + (i + 1) * exact, :] = term
                rest = rest - term.astype(jnp.float32)

    shape = jax.ShapeDtypeStruct((plain + 3 * exact, rank), jnp.bfloat16)
    return order.call(kernel, (pair, arrived), shape)


def data_rows(order, inputs, probe, piece, pieces, data):
    features = inputs.shape[0]
    tokens, rank = probe.shape
    tile = -(-features // 64) * 16
    tiles = pl.cdiv(features, tile) // pieces
    first = piece * tiles

    def kernel(x, p, *refs):
        refs[-1][...] = jnp.dot(x[...], p[...], preferred_element_type=jnp.float32)

    before = () if data is None else (data,)
    return order.call(
        kernel,
        (inputs, probe, *before),
        pltpu.HBM((features, rank), jnp.float32),
        vmem=52 * MIB,
        grid=(tiles,),
        in_specs=[
            pl.BlockSpec((tile, tokens), lambda i: (first + i, 0)),
            pl.BlockSpec((tokens, rank), lambda i: (0, 0)),
            *[ANYWHERE] * len(before),
        ],
        out_specs=[pl.BlockSpec((tile, rank), lambda i: (first + i, 0))],
        input_output_aliases={2: 0} if before else {},
    )


def data_parts(order, inputs, probe, after):
    tokens, rank = probe.shape
    quarter = inputs.shape[1] // 4
    shape = jax.ShapeDtypeStruct((2, quarter, rank), jnp.float32)
    out_spec = pl.BlockSpec((1, quarter, rank), lambda i: (i, 0, 0))

    def kernel(x, p, given, kept):
        odd = lax.axis_index("context") % 2 == 1
        product = token_contract(x[...], p[...])
        given[0] = jnp.where(odd, product[:quarter], product[quarter:])
        kept[0] = jnp.where(odd, product[quarter:], product[:quarter])

    return order.call(
        kernel,
        (inputs, probe),
        (shape, shape),
        after,
        vmem=52 * MIB,
        grid=(2,),
        in_specs=[
            pl.BlockSpec((tokens, 2 * quarter), lambda i: (0, i)),
            pl.BlockSpec((tokens, rank), lambda i: (0, 0)),
        ],
        out_specs=[out_spec, out_spec],
    )


def core_summed(order, kept, arrived):
    rows, rank = kept.shape[1:]

    def kernel(mine, theirs, stays, message, given):
        high = lax.select(lax.axis_index("context") >= 2, 1, 0)
        given[...] = mine[1 - high] + theirs[1 - high]
        stays[...] = mine[high] + theirs[high]
        pack(given, message, rows)

    shape = jax.ShapeDtypeStruct((rows, rank), jnp.float32)
    return order.call(
        kernel,
        (kept, arrived),
        (shape, packed_shape(shape, rows)),
        scratch_shapes=[pltpu.VMEM((rows, rank), jnp.float32)],
        vmem=12 * MIB,
    )


def finished(order, basis, eigen, cores, place, shares, scale):
    rows, rank = basis.shape
    part = cores.shape[0] // 4
    share = rank // 4

    def kernel(b, e, c, *refs):
        out = refs[-1]
        core = jnp.concatenate(
            [c[i * part + place * share : i * part + (place + 1) * share, :] for i in range(4)], 0
        )
        column = jnp.sum(jnp.where(diagonal(rank, rank), e[...], 0.0), axis=1, keepdims=True)
        rest = column * core
        prior = jnp.zeros((rows, rank), jnp.float32)
        for _ in range(3):
            term = rest.astype(jnp.bfloat16)
            prior += jnp.dot(b[...], term, preferred_element_type=jnp.float32)
            rest = rest - term.astype(jnp.float32)
        if len(refs) == 2:
            out[...] = 0.9 * prior + scale * refs[0][...]
        else:
            for start, stop, total in add_packed(refs[0], refs[1], rows):
                out[start:stop, :] = 0.9 * prior[start:stop] + scale * total

    shape = jax.ShapeDtypeStruct((rows, rank), jnp.float32)
    operands = (basis, eigen.reshape(1, rank), cores, *shares)
    return order.call(kernel, operands, shape, vmem=16 * MIB)


def core_parts(order, bases, omegas, after):
    rank = omegas[0].shape[1]
    share = rank // lax.axis_size("context")
    count = len(bases)

    def kernel(*refs):
        out, product = refs[-2:]
        start = pl.multiple_of(lax.axis_index("context") * share, share)
        for k in range(count):
            product[...] = token_contract(refs[k][...], refs[count + k][...])
            out[k * share : (k + 1) * share, :] = product[pl.ds(start, share), :]

    shape = jax.ShapeDtypeStruct((count * share, rank), jnp.float32)
    scratch = [pltpu.VMEM((rank, rank), jnp.float32)]
    return order.call(kernel, (*bases, *omegas), shape, after, 52 * MIB, scratch_shapes=scratch)


def lines_of_four(inputs, omegas, bases, eigens, scale):
    place = lax.axis_index("owner")
    inner = (place == 1) | (place == 2)
    turned = [x.shape[1] % 128 != 0 for x in inputs]
    inputs = [x.T if t else x for x, t in zip(inputs, turned)]
    order = Order()
    jobs = [k for k, _ in CHUNKS]
    count = len(jobs)
    partial, plain, message, inward, pair, across, probe, outward, chunk = (
        [None] * count for _ in range(9)
    )
    state = [None] * 3
    results = [None] * 3
    rank = omegas[0].shape[1]

    def multiply(i):
        k, share = CHUNKS[i]
        unit = inputs[k].shape[1 if turned[k] else 0] // 16
        start = unit * sum(n for j, n in CHUNKS[:i] if j == k)
        rows = unit * share
        partial[i] = probe_rows(order, inputs[k], omegas[k], start, rows, turned[k])
        if i == CARRIER:
            partial[i] = jnp.concatenate([partial[i], cores], 0)
        plain[i] = rows
        message[i] = packed(order, partial[i], rows)

    def send(i, after=()):
        if after:
            message[i] = order.gate(message[i], after)
        inward[i] = lax.ppermute(message[i], "owner", INWARD)

    def add_pair(i):
        pair[i], sums = paired(order, partial[i], inward[i], plain[i])
        across[i] = lax.ppermute(sums, "owner", ACROSS)

    def add_across(i):
        probe[i] = rounded(order, pair[i], across[i], plain[i])
        outward[i] = lax.ppermute(probe[i], "owner", OUTWARD)

    def carried(i):
        whole = lax.select(inner, probe[i], outward[i])
        if i != CARRIER:
            return whole, None
        terms = whole[plain[i] :].reshape(3, cores.shape[0], rank).astype(jnp.float32)
        return whole[: plain[i]], terms[0] + (terms[1] + terms[2])

    def probes(k):
        return jnp.concatenate([chunk[i] for i in range(count) if jobs[i] == k], 0)

    def contract(k, after=()):
        given, kept = data_parts(order, inputs[k], probes(k), after)
        state[k] = kept, given

    def share_out(k, now=False):
        if turned[k]:
            data = order.gate(state[k], (), True)
            state[k] = (lax.psum_scatter(data, "context", scatter_dimension=0, tiled=True),)
        else:
            kept, given = state[k]
            given = given if now else order.gate(given)
            state[k] = kept, lax.ppermute(given, "context", PAIRED)

    def add_cores(k):
        stays, given = core_summed(order, *state[k])
        state[k] = stays, lax.ppermute(given, "context", SKIPPED)

    def finish(k):
        results[k] = finished(order, picked[k], eigens[k], whole, k, state[k], scale)

    def receive(i):
        chunk[i], total = carried(i)
        return total

    def swapped(array, pairs, upper):
        theirs = lax.ppermute(order.gate(array), "context", pairs)
        return jnp.concatenate(
            [lax.select(upper, theirs, array), lax.select(upper, array, theirs)], 0
        )

    context = lax.axis_index("context")
    quarters = [b.shape[0] // 4 for b in bases]
    picked = [lax.dynamic_slice_in_dim(b, context * n, n, 0) for b, n in zip(bases, quarters)]
    multiply(0)
    send(0)
    multiply(1)
    for i in range(count):
        ahead = i + 1 < count
        shrinks = ahead and message[i].shape[0] > message[i + 1].shape[0]
        came = (inward[i],) if i < 2 else (inward[i], outward[i - 2])
        if shrinks:
            add_pair(i)
        if ahead:
            send(i + 1, came)
        if not shrinks:
            add_pair(i)
        if i > 0:
            add_across(i - 1)
        if i == 4:
            share_out(2)
            pairs = swapped(totals, PAIRED, context % 2 == 1)
        if i == 5:
            whole = swapped(pairs, SKIPPED, context >= 2)
        if i == CARRIER - 2:
            cores = core_parts(order, bases, omegas, picked)
        if i + 2 < count:
            multiply(i + 2)
        if i > 0:
            got = receive(i - 1)
            totals = got if i - 1 == CARRIER else totals if i > CARRIER + 1 else None
        if i in (2, 3):
            state[2] = data_rows(order, inputs[2], probes(2), i - 2, 2, state[2])
        if i == 4:
            contract(0)
    add_across(count - 1)
    share_out(0)
    add_cores(0)
    receive(count - 1)
    contract(1)
    share_out(1, True)
    add_cores(1)
    finish(2)
    finish(0)
    finish(1)
    return tuple(results)


def any_lines(inputs, omegas, bases, eigens, scale):
    cores = core_total(bases, omegas)
    results = []
    for x, w, b, e, core in zip(inputs, omegas, bases, eigens, cores):
        partial = jnp.dot(x, w, preferred_element_type=jnp.float32)
        share = lax.psum_scatter(partial, "owner", scatter_dimension=0, tiled=True)
        probe = lax.all_gather(share.astype(jnp.bfloat16), "owner", axis=0, tiled=True)
        data = lax.psum_scatter(
            token_contract(x, probe), "context", scatter_dimension=0, tiled=True
        )
        results.append(prior_rows(b, e, core) + scale * data)
    return tuple(results)


def per_device(
    x_attn,
    x_mlp,
    x_down,
    omega_attn,
    omega_mlp,
    omega_down,
    basis_attn,
    basis_mlp,
    basis_down,
    eig_attn,
    eig_mlp,
    eig_down,
):
    inputs = (x_attn, x_mlp, x_down)
    omegas = (omega_attn, omega_mlp, omega_down)
    bases = (basis_attn, basis_mlp, basis_down)
    eigens = (eig_attn, eig_mlp, eig_down)
    scale = 0.1 / (x_attn.shape[0] * lax.axis_size("context"))
    fours = lax.axis_size("owner") == 4 and lax.axis_size("context") == 4
    run = lines_of_four if fours else any_lines
    return run(inputs, omegas, bases, eigens, scale)


def solution(mesh):
    placed = (
        P(("section", "context"), "owner"),
        P(("section", "context"), "owner"),
        P(("section", "context"), "owner"),
        P(("section", "owner"), None),
        P(("section", "owner"), None),
        P(("section", "owner"), None),
        P(("section", "owner"), None),
        P(("section", "owner"), None),
        P(("section", "owner"), None),
        P("section"),
        P("section"),
        P("section"),
    )
    return jax.shard_map(
        per_device,
        mesh=mesh,
        in_specs=placed,
        out_specs=(
            P(("section", "owner", "context"), None),
            P(("section", "owner", "context"), None),
            P(("section", "owner", "context"), None),
        ),
        check_vma=False,
    )
```

time: 302 us -> 234 us (0.77)
  waiting for transfers between devices: 116 us -> 54.3 us
  Pallas kernels: 65.6 us -> 95.4 us
  starting transfers between devices: 64.7 us -> 49.2 us
  blocking collectives: 13.3 us -> 0 us
  matrix products: 4.87 us -> 0 us
    ppermute x26 -> x22, waiting for transfers between devices: 94.9 us -> 46.2 us  [the longest x6 25.4 us: add_across(): outward[i] = lax.ppermute(probe[i], 'owner', OUTWARD)]
    pallas_call x32 -> x43, Pallas kernels: 65.6 us -> 95.4 us  [call(): pl.pallas_call(body, out_shape=(*outs, jax.ShapeDtypeStruct((8, 128), jnp...]
    ppermute x26 -> x22, starting transfers between devices: 62.1 us -> 47.1 us  [the longest x6 30.2 us: send(): inward[i] = lax.ppermute(message[i], 'owner', INWARD)]
    all_gather x1 -> x0, blocking collectives: 13.3 us -> none  [lines_of_four(): lax.all_gather(total, 'context', axis=0).reshape(4, 3, rank // 4, rank)]
    ppermute x2, waiting for transfers between devices: 20.7 us -> 8.04 us  [add_cores(): state[k] = (stays, lax.ppermute(given, 'context', SKIPPED))]
    dot_general x3 -> x0, matrix products: 4.87 us -> none  [prior_rows(): jnp.dot(picked.astype(jnp.float32), weighted, precision=lax.Precision.HIG...]
    unnamed x48 -> x61, local copies, waits for them, and re-layouts: 13.8 us -> 10.4 us
  transfers between devices with their start and end apart: 29 -> 25, of which waited for: 10 -> 10; matrix products, arithmetic and copies ran while one was open for 3% -> 4% of each run, Pallas kernels for 15% -> 35%
where the time goes in v2:
time: 234 us; the launch traced here: 232 us
  Pallas kernels  95.4 us (41%)
  waiting for transfers between devices  54.3 us (23%)
  starting transfers between devices  49.2 us (21%)
  between operations  14.6 us (6%)
  local copies, waits for them, and re-layouts  12.8 us (5%)
  other arithmetic  6.08 us (3%)
    pallas_call x43, Pallas kernels, call(): pl.pallas_call(body, out_shape=(*outs, jax.ShapeDtypeStruct((8, 128), jnp...  95.4 us
    ppermute x6, starting transfers between devices, send(): inward[i] = lax.ppermute(message[i], 'owner', INWARD)  30.2 us
    ppermute x6, waiting for transfers between devices, add_across(): outward[i] = lax.ppermute(probe[i], 'owner', OUTWARD)  25.4 us
    ppermute x6, waiting for transfers between devices, send(): inward[i] = lax.ppermute(message[i], 'owner', INWARD)  15.3 us
    unnamed x61, local copies, waits for them, and re-layouts  10.4 us
    ppermute x6, starting transfers between devices, add_across(): outward[i] = lax.ppermute(probe[i], 'owner', OUTWARD)  8.17 us
    ppermute x2, waiting for transfers between devices, add_cores(): state[k] = (stays, lax.ppermute(given, 'context', SKIPPED))  8.04 us
    ppermute x6, starting transfers between devices, add_pair(): across[i] = lax.ppermute(sums, 'owner', ACROSS)  6.76 us
  transfers between devices with their start and end apart: 25, of which 10 were waited for; matrix products, arithmetic and copies ran while one was open for 4% of the time, Pallas kernels for 35%

profile of v2, /device:TPU:0, one launch (start us, length us, event | category | flops | bytes accessed | tf_op | source)
XLA Modules:
  0.0 232.5 jit_solution(17214565800727543931)
XLA Ops:
  7.2 8.6 %shard_map.139 = (f32[1024,256]{1,0:T(8,128)S(1)}, f32[8,128]{1,0:T(8,128)S(1)}) custom-call(bf16[7392,2048]{1,0:T(8,128)(2,1)} %bitcast.7, bf16[7392,256]{1,0:T(8,128)(2,1)} %refs_5_.1), custom_call_target="tpu_custom_call" | custom-call | tf_op jit(solution)/shard_map/pallas_call | solution.py:70
  16.2 5.0 %collective-permute-start = (f32[696,256]{1,0:T(8,128)S(1)}, f32[696,256]{1,0:T(8,128)S(1)}, u32[]{:S(2)}, u32[]{:S(2)}) collective-permute-start(f32[696,256]{1,0:T(8,128)S(1)} %get-tuple-element.100), channel_id=1, source_target_pairs={{0,4},{12,8},{1,5},{13,9},{2,6},{14,10},{3,7},{15,11},{16,20},{28,... | collective-permute-start | bytes 2138120 | tf_op jit(solution)/shard_map/ppermute | solution.py:372
  21.2 8.7 %shard_map.141 = (f32[1024,256]{1,0:T(8,128)S(1)}, f32[8,128]{1,0:T(8,128)S(1)}) custom-call(bf16[7392,2048]{1,0:T(8,128)(2,1)} %bitcast.8, bf16[7392,256]{1,0:T(8,128)(2,1)} %refs_5_.1, f32[8,128]{1,0:T(8,128)S(1)} %get-tuple-element.101.refs_2_), custom_call_target="tpu_custom_call" | custom-call | tf_op jit(solution)/shard_map/pallas_call | solution.py:70
  31.2 5.2 %collective-permute-done.refs_2_.refs_1_ = f32[696,256]{1,0:T(8,128)S(1)} collective-permute-done((f32[696,256]{1,0:T(8,128)S(1)}, f32[696,256]{1,0:T(8,128)S(1)}, u32[]{:S(2)}, u32[]{:S(2)}) %collective-permute-start) | collective-permute-done | bytes 712736 | tf_op jit(solution)/shard_map/ppermute | solution.py:372
  36.4 4.4 %collective-permute-start.1 = (f32[696,256]{1,0:T(8,128)}, f32[696,256]{1,0:T(8,128)S(1)}, u32[]{:S(2)}, u32[]{:S(2)}) collective-permute-start(f32[696,256]{1,0:T(8,128)} %get-tuple-element.114), channel_id=1, source_target_pairs={{0,4},{12,8},{1,5},{13,9},{2,6},{14,10},{3,7},{15,11},{16,20},{28,... | collective-permute-start | bytes 2138120 | tf_op jit(solution)/shard_map/ppermute | solution.py:372
  45.9 6.2 %shard_map.145 = (f32[192,256]{1,0:T(8,128)S(1)}, f32[8,128]{1,0:T(8,128)S(1)}) custom-call(bf16[2048,256]{1,0:T(8,128)(2,1)} %refs_0_.7, bf16[2048,256]{1,0:T(8,128)(2,1)} %refs_1_.9, bf16[7392,256]{1,0:T(8,128)(2,1)} %refs_2_.1, bf16[2048,256]{1,0:T(8,128)(2,1)} %refs_1_.11, bf16[2048,256]{1,0:T(8,128)(2,1)} %refs_1_.13, bf16[7392,256]{1,0:T(8,128)(2,1)} %refs_5_.1, ...), custom_call_target="tpu_custom_call" | custom-call | tf_op jit(solution)/shard_map/pallas_call | solution.py:70
  52.1 3.3 %shard_map.146 = (f32[1024,256]{1,0:T(8,128)S(1)}, f32[8,128]{1,0:T(8,128)S(1)}) custom-call(bf16[2048,2048]{1,0:T(8,128)(2,1)} %refs_0_.12, bf16[2048,256]{1,0:T(8,128)(2,1)} %refs_1_.11, f32[8,128]{1,0:T(8,128)S(1)} %get-tuple-element.108.refs_2_), custom_call_target="tpu_custom_call" | custom-call | tf_op jit(solution)/shard_map/pallas_call | solution.py:70
  56.0 4.1 %collective-permute-start.2 = (f32[888,256]{1,0:T(8,128)S(1)}, f32[888,256]{1,0:T(8,128)S(1)}, u32[]{:S(2)}, u32[]{:S(2)}) collective-permute-start(f32[888,256]{1,0:T(8,128)S(1)} %get-tuple-element.115), channel_id=1, source_target_pairs={{0,4},{12,8},{1,5},{13,9},{2,6},{14,10},{3,7},{15,11},{16,20},{28,... | collective-permute-start | bytes 2727944 | tf_op jit(solution)/shard_map/ppermute | solution.py:372
  64.4 3.3 %shard_map.151 = (f32[1024,256]{1,0:T(8,128)S(1)}, f32[8,128]{1,0:T(8,128)S(1)}) custom-call(bf16[2048,2048]{1,0:T(8,128)(2,1)} %refs_0_.12, bf16[2048,256]{1,0:T(8,128)(2,1)} %refs_1_.11, f32[8,128]{1,0:T(8,128)S(1)} %get-tuple-element.120.refs_2_), custom_call_target="tpu_custom_call" | custom-call | tf_op jit(solution)/shard_map/pallas_call | solution.py:70
  68.1 10.2 %collective-permute-done.2.refs_1_.refs_2_ = f32[888,256]{1,0:T(8,128)S(1)} collective-permute-done((f32[888,256]{1,0:T(8,128)S(1)}, f32[888,256]{1,0:T(8,128)S(1)}, u32[]{:S(2)}, u32[]{:S(2)}) %collective-permute-start.2) | collective-permute-done | bytes 909344 | tf_op jit(solution)/shard_map/ppermute | solution.py:372
  85.2 6.3 %collective-permute-start.6 = (f32[696,256]{1,0:T(8,128)}, f32[696,256]{1,0:T(8,128)S(1)}, u32[]{:S(2)}, u32[]{:S(2)}) collective-permute-start(f32[696,256]{1,0:T(8,128)} %copy-done.14), channel_id=1, source_target_pairs={{0,4},{12,8},{1,5},{13,9},{2,6},{14,10},{3,7},{15,11},{16,20},{28,... | collective-permute-start | bytes 2138120 | tf_op jit(solution)/shard_map/ppermute | solution.py:372
  91.6 3.3 %shard_map.156 = (f32[1024,256]{1,0:T(8,128)S(1)}, f32[8,128]{1,0:T(8,128)S(1)}) custom-call(bf16[2048,2048]{1,0:T(8,128)(2,1)} %refs_0_.13, bf16[2048,256]{1,0:T(8,128)(2,1)} %refs_1_.13, f32[8,128]{1,0:T(8,128)S(1)} %get-tuple-element.133.refs_2_), custom_call_target="tpu_custom_call" | custom-call | tf_op jit(solution)/shard_map/pallas_call | solution.py:70
  97.4 8.8 %shard_map.158 = (f32[7392,256]{1,0:T(8,128)}, f32[8,128]{1,0:T(8,128)S(1)}) custom-call(bf16[7392,2048]{1,0:T(8,128)(2,1)} %bitcast.9, bf16[2048,256]{1,0:T(8,128)(2,1)S(1)} %pad_maximum_fusion.refs_1_, f32[8,128]{1,0:T(8,128)S(1)} %get-tuple-element.138.refs_2_), custom_call_target="tpu_custom_call" | custom-call | tf_op jit(solution)/shard_map/pallas_call | solution.py:70
  110.9 4.6 %collective-permute-start.11 = (f32[696,256]{1,0:T(8,128)S(1)}, f32[696,256]{1,0:T(8,128)S(1)}, u32[]{:S(2)}, u32[]{:S(2)}) collective-permute-start(f32[696,256]{1,0:T(8,128)S(1)} %get-tuple-element.151), channel_id=1, source_target_pairs={{0,4},{12,8},{1,5},{13,9},{2,6},{14,10},{3,7},{15,11},{16,20},{28,... | collective-permute-start | bytes 2138120 | tf_op jit(solution)/shard_map/ppermute | solution.py:372
  116.3 3.3 %shard_map.162 = (f32[1024,256]{1,0:T(8,128)S(1)}, f32[8,128]{1,0:T(8,128)S(1)}) custom-call(bf16[2048,2048]{1,0:T(8,128)(2,1)} %refs_0_.13, bf16[2048,256]{1,0:T(8,128)(2,1)} %refs_1_.13, f32[8,128]{1,0:T(8,128)S(1)} %get-tuple-element.144.refs_2_), custom_call_target="tpu_custom_call" | custom-call | tf_op jit(solution)/shard_map/pallas_call | solution.py:70
  120.0 8.8 %shard_map.164 = (f32[7392,256]{1,0:T(8,128)}, f32[8,128]{1,0:T(8,128)S(1)}) custom-call(bf16[7392,2048]{1,0:T(8,128)(2,1)} %bitcast.10, bf16[2048,256]{1,0:T(8,128)(2,1)S(1)} %pad_maximum_fusion.refs_1_, f32[7392,256]{1,0:T(8,128)} %get-tuple-element.143.refs_2_, f32[8,128]{1,0:T(8,128)S(1)} %get-tuple-element.147.refs_3_), custom_call_target="tpu_custom_call", output_to_operand_aliasing={{0}: (2, {})} | custom-call | tf_op jit(solution)/shard_map/pallas_call | solution.py:70
  133.4 5.8 %collective-permute-start.14 = (f32[696,256]{1,0:T(8,128)S(1)}, f32[696,256]{1,0:T(8,128)S(1)}, u32[]{:S(2)}, u32[]{:S(2)}) collective-permute-start(f32[696,256]{1,0:T(8,128)S(1)} %copy-done.16), channel_id=1, source_target_pairs={{0,4},{12,8},{1,5},{13,9},{2,6},{14,10},{3,7},{15,11},{16,20},{28,... | collective-permute-start | bytes 2138120 | tf_op jit(solution)/shard_map/ppermute | solution.py:372
  140.8 3.5 %collective-permute-done.15 = bf16[1024,256]{1,0:T(8,128)(2,1)S(1)} collective-permute-done((bf16[1024,256]{1,0:T(8,128)(2,1)}, bf16[1024,256]{1,0:T(8,128)(2,1)S(1)}, u32[]{:S(2)}, u32[]{:S(2)}) %collective-permute-start.15) | collective-permute-done | bytes 524320 | tf_op jit(solution)/shard_map/ppermute | solution.py:380
  145.4 6.3 %shard_map.170 = (f32[2,512,256]{2,1,0:T(8,128)S(1)}, f32[2,512,256]{2,1,0:T(8,128)}, f32[8,128]{1,0:T(8,128)S(1)}) custom-call(bf16[2048,2048]{1,0:T(8,128)(2,1)} %refs_0_.12, bf16[2048,256]{1,0:T(8,128)(2,1)} %pad_maximum_fusion.1.refs_1_, f32[8,128]{1,0:T(8,128)S(1)} %get-tuple-element.163.refs_2_), custom_call_target="tpu_custom_call" | custom-call | tf_op jit(solution)/shard_map/pallas_call | solution.py:70
  165.6 9.6 %collective-permute-done.20 = bf16[1024,256]{1,0:T(8,128)(2,1)S(1)} collective-permute-done((bf16[1024,256]{1,0:T(8,128)(2,1)S(1)}, bf16[1024,256]{1,0:T(8,128)(2,1)S(1)}, u32[]{:S(2)}, u32[]{:S(2)}) %collective-permute-start.20) | collective-permute-done | bytes 524320 | tf_op jit(solution)/shard_map/ppermute | solution.py:380
  175.3 11.4 %collective-permute-done.21 = bf16[1024,256]{1,0:T(8,128)(2,1)S(1)} collective-permute-done((bf16[1024,256]{1,0:T(8,128)(2,1)S(1)}, bf16[1024,256]{1,0:T(8,128)(2,1)S(1)}, u32[]{:S(2)}, u32[]{:S(2)}) %collective-permute-start.21) | collective-permute-done | bytes 524320 | tf_op jit(solution)/shard_map/ppermute | solution.py:380
  189.6 6.2 %shard_map.177 = (f32[2,512,256]{2,1,0:T(8,128)}, f32[2,512,256]{2,1,0:T(8,128)}, f32[8,128]{1,0:T(8,128)S(1)}) custom-call(bf16[2048,2048]{1,0:T(8,128)(2,1)} %refs_0_.13, bf16[2048,256]{1,0:T(8,128)(2,1)} %pad_maximum_fusion.2.refs_1_, f32[8,128]{1,0:T(8,128)S(1)} %get-tuple-element.181.refs_2_), custom_call_target="tpu_custom_call" | custom-call | tf_op jit(solution)/shard_map/pallas_call | solution.py:70
  203.3 4.6 %collective-permute-done.16 = f32[384,256]{1,0:T(8,128)} collective-permute-done((f32[384,256]{1,0:T(8,128)S(1)}, f32[384,256]{1,0:T(8,128)}, u32[]{:S(2)}, u32[]{:S(2)}) %collective-permute-start.16) | collective-permute-done | bytes 393248 | tf_op jit(solution)/shard_map/ppermute | solution.py:417
  218.1 5.2 %collective-permute-done.23.refs_4_ = f32[360,256]{1,0:T(8,128)} collective-permute-done((f32[360,256]{1,0:T(8,128)}, f32[360,256]{1,0:T(8,128)}, u32[]{:S(2)}, u32[]{:S(2)}) %collective-permute-start.23) | collective-permute-done | bytes 368672 | tf_op jit(solution)/shard_map/ppermute | solution.py:407
  (150 shorter events, 71.0 us)
Async XLA Ops:
  7.2 201.9 %reduce-scatter.2.cloned.1.call-start = ((), (), s32[]{:S(2)}) async-start(), calls=%async_computation.1 | async-start | bytes 9461760 | tf_op jit(solution)/shard_map/reduce_scatter | solution.py:399
  16.2 20.1 %collective-permute-start = (f32[696,256]{1,0:T(8,128)S(1)}, f32[696,256]{1,0:T(8,128)S(1)}, u32[]{:S(2)}, u32[]{:S(2)}) collective-permute-start(f32[696,256]{1,0:T(8,128)S(1)} %get-tuple-element.100), channel_id=1, source_target_pairs={{0,4},{12,8},{1,5},{13,9},{2,6},{14,10},{3,7},{15,11},{16,20},{28,... | collective-permute-start | bytes 2138120 | tf_op jit(solution)/shard_map/ppermute | solution.py:372
  36.4 19.6 %collective-permute-start.1 = (f32[696,256]{1,0:T(8,128)}, f32[696,256]{1,0:T(8,128)S(1)}, u32[]{:S(2)}, u32[]{:S(2)}) collective-permute-start(f32[696,256]{1,0:T(8,128)} %get-tuple-element.114), channel_id=1, source_target_pairs={{0,4},{12,8},{1,5},{13,9},{2,6},{14,10},{3,7},{15,11},{16,20},{28,... | collective-permute-start | bytes 2138120 | tf_op jit(solution)/shard_map/ppermute | solution.py:372
  44.1 18.3 %collective-permute-start.3 = (f32[696,256]{1,0:T(8,128)S(1)}, f32[696,256]{1,0:T(8,128)S(1)}, u32[]{:S(2)}, u32[]{:S(2)}) collective-permute-start(f32[696,256]{1,0:T(8,128)S(1)} %get-tuple-element.117), channel_id=1, source_target_pairs={{4,8},{8,4},{5,9},{9,5},{6,10},{10,6},{7,11},{11,7},{20,24},{24,20... | collective-permute-start | bytes 2138120 | tf_op jit(solution)/shard_map/ppermute | solution.py:376
  56.0 22.3 %collective-permute-start.2 = (f32[888,256]{1,0:T(8,128)S(1)}, f32[888,256]{1,0:T(8,128)S(1)}, u32[]{:S(2)}, u32[]{:S(2)}) collective-permute-start(f32[888,256]{1,0:T(8,128)S(1)} %get-tuple-element.115), channel_id=1, source_target_pairs={{0,4},{12,8},{1,5},{13,9},{2,6},{14,10},{3,7},{15,11},{16,20},{28,... | collective-permute-start | bytes 2727944 | tf_op jit(solution)/shard_map/ppermute | solution.py:372
  61.7 19.3 %collective-permute-start.7 = (f32[696,256]{1,0:T(8,128)}, f32[696,256]{1,0:T(8,128)S(1)}, u32[]{:S(2)}, u32[]{:S(2)}) collective-permute-start(f32[696,256]{1,0:T(8,128)} %get-tuple-element.131), channel_id=1, source_target_pairs={{4,8},{8,4},{5,9},{9,5},{6,10},{10,6},{7,11},{11,7},{20,24},{24,20... | collective-permute-start | bytes 2138120 | tf_op jit(solution)/shard_map/ppermute | solution.py:376
  62.9 18.1 %collective-permute-start.5 = (bf16[1024,256]{1,0:T(8,128)(2,1)S(1)}, bf16[1024,256]{1,0:T(8,128)(2,1)S(1)}, u32[]{:S(2)}, u32[]{:S(2)}) collective-permute-start(bf16[1024,256]{1,0:T(8,128)(2,1)S(1)} %get-tuple-element.128), channel_id=1, source_target_pairs={{4,0},{8,12},{5,1},{9,13},{6,2},{10,14},{7,3},{11,15},{20,16},{24,... | collective-permute-start | bytes 1572872 | tf_op jit(solution)/shard_map/ppermute | solution.py:380
  82.3 13.9 %collective-permute-start.8 = (bf16[1024,256]{1,0:T(8,128)(2,1)}, bf16[1024,256]{1,0:T(8,128)(2,1)}, u32[]{:S(2)}, u32[]{:S(2)}) collective-permute-start(bf16[1024,256]{1,0:T(8,128)(2,1)} %get-tuple-element.137), channel_id=1, source_target_pairs={{4,0},{8,12},{5,1},{9,13},{6,2},{10,14},{7,3},{11,15},{20,16},{24,... | collective-permute-start | bytes 1572872 | tf_op jit(solution)/shard_map/ppermute | solution.py:380
  83.6 24.3 %collective-permute-start.4 = (f32[888,256]{1,0:T(8,128)}, f32[888,256]{1,0:T(8,128)}, u32[]{:S(2)}, u32[]{:S(2)}) collective-permute-start(f32[888,256]{1,0:T(8,128)} %get-tuple-element.125), channel_id=1, source_target_pairs={{4,8},{8,4},{5,9},{9,5},{6,10},{10,6},{7,11},{11,7},{20,24},{24,20... | collective-permute-start | bytes 2727944 | tf_op jit(solution)/shard_map/ppermute | solution.py:376
  85.2 21.0 %collective-permute-start.6 = (f32[696,256]{1,0:T(8,128)}, f32[696,256]{1,0:T(8,128)S(1)}, u32[]{:S(2)}, u32[]{:S(2)}) collective-permute-start(f32[696,256]{1,0:T(8,128)} %copy-done.14), channel_id=1, source_target_pairs={{0,4},{12,8},{1,5},{13,9},{2,6},{14,10},{3,7},{15,11},{16,20},{28,... | collective-permute-start | bytes 2138120 | tf_op jit(solution)/shard_map/ppermute | solution.py:372
  109.6 19.2 %collective-permute-start.9 = (bf16[1600,256]{1,0:T(8,128)(2,1)S(1)}, bf16[1600,256]{1,0:T(8,128)(2,1)S(1)}, u32[]{:S(2)}, u32[]{:S(2)}) collective-permute-start(bf16[1600,256]{1,0:T(8,128)(2,1)S(1)} %get-tuple-element.142), channel_id=1, source_target_pairs={{4,0},{8,12},{5,1},{9,13},{6,2},{10,14},{7,3},{11,15},{20,16},{24,... | collective-permute-start | bytes 2457608 | tf_op jit(solution)/shard_map/ppermute | solution.py:380
  110.9 17.9 %collective-permute-start.11 = (f32[696,256]{1,0:T(8,128)S(1)}, f32[696,256]{1,0:T(8,128)S(1)}, u32[]{:S(2)}, u32[]{:S(2)}) collective-permute-start(f32[696,256]{1,0:T(8,128)S(1)} %get-tuple-element.151), channel_id=1, source_target_pairs={{0,4},{12,8},{1,5},{13,9},{2,6},{14,10},{3,7},{15,11},{16,20},{28,... | collective-permute-start | bytes 2138120 | tf_op jit(solution)/shard_map/ppermute | solution.py:372
  115.6 14.9 %collective-permute-start.10 = (f32[696,256]{1,0:T(8,128)}, f32[696,256]{1,0:T(8,128)S(1)}, u32[]{:S(2)}, u32[]{:S(2)}) collective-permute-start(f32[696,256]{1,0:T(8,128)} %get-tuple-element.150), channel_id=1, source_target_pairs={{4,8},{8,4},{5,9},{9,5},{6,10},{10,6},{7,11},{11,7},{20,24},{24,20... | collective-permute-start | bytes 2138120 | tf_op jit(solution)/shard_map/ppermute | solution.py:376
  131.8 12.5 %collective-permute-start.15 = (bf16[1024,256]{1,0:T(8,128)(2,1)}, bf16[1024,256]{1,0:T(8,128)(2,1)S(1)}, u32[]{:S(2)}, u32[]{:S(2)}) collective-permute-start(bf16[1024,256]{1,0:T(8,128)(2,1)} %copy-done.22), channel_id=1, source_target_pairs={{4,0},{8,12},{5,1},{9,13},{6,2},{10,14},{7,3},{11,15},{20,16},{24,... | collective-permute-start | bytes 1572872 | tf_op jit(solution)/shard_map/ppermute | solution.py:380
  133.4 18.4 %collective-permute-start.14 = (f32[696,256]{1,0:T(8,128)S(1)}, f32[696,256]{1,0:T(8,128)S(1)}, u32[]{:S(2)}, u32[]{:S(2)}) collective-permute-start(f32[696,256]{1,0:T(8,128)S(1)} %copy-done.16), channel_id=1, source_target_pairs={{0,4},{12,8},{1,5},{13,9},{2,6},{14,10},{3,7},{15,11},{16,20},{28,... | collective-permute-start | bytes 2138120 | tf_op jit(solution)/shard_map/ppermute | solution.py:372
  139.2 16.7 %collective-permute-start.13 = (f32[696,256]{1,0:T(8,128)}, f32[696,256]{1,0:T(8,128)}, u32[]{:S(2)}, u32[]{:S(2)}) collective-permute-start(f32[696,256]{1,0:T(8,128)} %get-tuple-element.160), channel_id=1, source_target_pairs={{4,8},{8,4},{5,9},{9,5},{6,10},{10,6},{7,11},{11,7},{20,24},{24,20... | collective-permute-start | bytes 2138120 | tf_op jit(solution)/shard_map/ppermute | solution.py:376
  154.4 7.8 %collective-permute-start.17 = (f32[696,256]{1,0:T(8,128)}, f32[696,256]{1,0:T(8,128)}, u32[]{:S(2)}, u32[]{:S(2)}) collective-permute-start(f32[696,256]{1,0:T(8,128)} %get-tuple-element.171), channel_id=1, source_target_pairs={{4,8},{8,4},{5,9},{9,5},{6,10},{10,6},{7,11},{11,7},{20,24},{24,20... | collective-permute-start | bytes 2138120 | tf_op jit(solution)/shard_map/ppermute | solution.py:376
  155.9 4.4 %collective-permute-start.12 = (f32[192,256]{1,0:T(8,128)S(1)}, f32[192,256]{1,0:T(8,128)S(1)}, u32[]{:S(2)}, u32[]{:S(2)}) collective-permute-start(f32[192,256]{1,0:T(8,128)S(1)} %get-tuple-element.158), channel_id=1, source_target_pairs={{0,1},{1,0},{2,3},{3,2},{4,5},{5,4},{6,7},{7,6},{8,9},{9,8},{10,11... | collective-permute-start | bytes 589832 | tf_op jit(solution)/shard_map/ppermute | solution.py:417
  158.8 16.4 %collective-permute-start.20 = (bf16[1024,256]{1,0:T(8,128)(2,1)S(1)}, bf16[1024,256]{1,0:T(8,128)(2,1)S(1)}, u32[]{:S(2)}, u32[]{:S(2)}) collective-permute-start(bf16[1024,256]{1,0:T(8,128)(2,1)S(1)} %get-tuple-element.179), channel_id=1, source_target_pairs={{4,0},{8,12},{5,1},{9,13},{6,2},{10,14},{7,3},{11,15},{20,16},{24,... | collective-permute-start | bytes 1572872 | tf_op jit(solution)/shard_map/ppermute | solution.py:380
  163.7 24.1 %collective-permute-start.18 = (f32[2,512,256]{2,1,0:T(8,128)S(1)}, f32[2,512,256]{2,1,0:T(8,128)S(1)}, u32[]{:S(2)}, u32[]{:S(2)}) collective-permute-start(f32[2,512,256]{2,1,0:T(8,128)S(1)} %get-tuple-element.174), channel_id=1, source_target_pairs={{0,1},{1,0},{2,3},{3,2},{4,5},{5,4},{6,7},{7,6},{8,9},{9,8},{10,11... | collective-permute-start | bytes 3145736 | tf_op jit(solution)/shard_map/ppermute | solution.py:403
  164.3 22.4 %collective-permute-start.21 = (bf16[1024,256]{1,0:T(8,128)(2,1)S(1)}, bf16[1024,256]{1,0:T(8,128)(2,1)S(1)}, u32[]{:S(2)}, u32[]{:S(2)}) collective-permute-start(bf16[1024,256]{1,0:T(8,128)(2,1)S(1)} %get-tuple-element.180), channel_id=1, source_target_pairs={{4,0},{8,12},{5,1},{9,13},{6,2},{10,14},{7,3},{11,15},{20,16},{24,... | collective-permute-start | bytes 1572872 | tf_op jit(solution)/shard_map/ppermute | solution.py:380
  195.9 12.0 %collective-permute-start.16 = (f32[384,256]{1,0:T(8,128)S(1)}, f32[384,256]{1,0:T(8,128)}, u32[]{:S(2)}, u32[]{:S(2)}) collective-permute-start(f32[384,256]{1,0:T(8,128)S(1)} %get-tuple-element.167), channel_id=1, source_target_pairs={{0,2},{2,0},{1,3},{3,1},{4,6},{6,4},{5,7},{7,5},{8,10},{10,8},{9,1... | collective-permute-start | bytes 1179656 | tf_op jit(solution)/shard_map/ppermute | solution.py:417
  197.3 18.5 %collective-permute-start.19 = (f32[360,256]{1,0:T(8,128)}, f32[360,256]{1,0:T(8,128)}, u32[]{:S(2)}, u32[]{:S(2)}) collective-permute-start(f32[360,256]{1,0:T(8,128)} %get-tuple-element.177), channel_id=1, source_target_pairs={{0,2},{2,0},{1,3},{3,1},{4,6},{6,4},{5,7},{7,5},{8,10},{10,8},{9,1... | collective-permute-start | bytes 1105928 | tf_op jit(solution)/shard_map/ppermute | solution.py:407
  201.8 21.5 %collective-permute-start.23 = (f32[360,256]{1,0:T(8,128)}, f32[360,256]{1,0:T(8,128)}, u32[]{:S(2)}, u32[]{:S(2)}) collective-permute-start(f32[360,256]{1,0:T(8,128)} %get-tuple-element.189), channel_id=1, source_target_pairs={{0,2},{2,0},{1,3},{3,1},{4,6},{6,4},{5,7},{7,5},{8,10},{10,8},{9,1... | collective-permute-start | bytes 1105928 | tf_op jit(solution)/shard_map/ppermute | solution.py:407
  (31 other events, 168.3 us)
Sparse Core Ops, SparseCore 0:
  131.9 66.6 reduce-scatter.1

commit v3 on v2

--- a/solution.py
+++ b/solution.py
@@ -14,6 +14,16 @@
 SKIPPED = ((0, 2), (2, 0), (1, 3), (3, 1))
 CHUNKS = ((2, 8), (2, 8), (0, 8), (0, 8), (1, 8), (1, 8))
 CARRIER = 2
+TERMS = 3
+STEPS = ("GB", "GBR", "BGR", "GBR", "GBR", "BR")
+SWAPS, SHARED, ATTN, PIECES = (4, 4), 4, 4, (2, 3)
+WAITS = 1
+SELECTED = True
+FENCED = False
+ROOM = 52
+SPLIT = 2
+SUMMED = 5
+EARLY = 2
 FINE, COARSE = 65535.0, 32500.0
 MIB = 1024 * 1024
 FIRST = (((0,), (0,)), ((), ()))
@@ -72,6 +82,7 @@
             out_shape=(*outs, jax.ShapeDtypeStruct((8, 128), jnp.float32)),
             in_specs=[*specs, *[ANYWHERE] * len(held)],
             out_specs=[*out_specs, marked],
+            cost_estimate=pl.CostEstimate(flops=10**9, bytes_accessed=10**7, transcendentals=0),
             compiler_params=pltpu.CompilerParams(vmem_limit_bytes=vmem),
             **rest,
         )(*operands, *held)
@@ -92,8 +103,9 @@
 
 
 def probe_rows(order, inputs, omega, start, rows, turned):
+    depth, rank = omega.shape
+    shape = jax.ShapeDtypeStruct((rows, rank), jnp.float32)
     tile = math.gcd(512, start, rows)
-    rank = omega.shape[1]
     first = start // tile
 
     def kernel(x, w, out):
@@ -102,7 +114,6 @@
         else:
             out[...] = jnp.dot(x[...], w[...], preferred_element_type=jnp.float32)
 
-    depth = omega.shape[0]
     if turned:
         spec = pl.BlockSpec((depth, tile), lambda i: (0, first + i))
     else:
@@ -110,8 +121,8 @@
     return order.call(
         kernel,
         (inputs, omega),
-        jax.ShapeDtypeStruct((rows, rank), jnp.float32),
-        vmem=52 * MIB,
+        shape,
+        vmem=ROOM * MIB,
         grid=(rows // tile,),
         in_specs=[spec, pl.BlockSpec((depth, rank), lambda i: (0, 0))],
         out_specs=[pl.BlockSpec((tile, rank), lambda i: (i, 0))],
@@ -186,10 +197,9 @@
     return jax.ShapeDtypeStruct((rows, value.shape[1]), jnp.float32)
 
 
-def packed(order, partial, plain):
-    return order.call(
-        lambda value, out: pack(value, out, plain), (partial,), packed_shape(partial, plain)
-    )
+def packed(order, partial, plain, after):
+    shape = packed_shape(partial, plain)
+    return order.call(lambda value, out: pack(value, out, plain), (partial,), shape, after)
 
 
 def paired(order, partial, arrived, plain):
@@ -204,7 +214,7 @@
     return order.call(kernel, (partial, arrived), (shape, packed_shape(partial, plain)))
 
 
-def rounded(order, pair, arrived, plain):
+def rounded(order, pair, arrived, plain, after):
     rows, rank = pair.shape
     exact = rows - plain
 
@@ -213,66 +223,112 @@
             out[start:stop, :] = total.astype(jnp.bfloat16)
         if exact:
             rest = mine[plain:, :] + theirs[2 * third(plain) + 8 :, :]
-            for i in range(3):
+            for i in range(TERMS):
                 term = rest.astype(jnp.bfloat16)
                 out[plain + i * exact : plain + (i + 1) * exact, :] = term
                 rest = rest - term.astype(jnp.float32)
 
-    shape = jax.ShapeDtypeStruct((plain + 3 * exact, rank), jnp.bfloat16)
-    return order.call(kernel, (pair, arrived), shape)
-
-
-def data_rows(order, inputs, probe, piece, pieces, data):
-    features = inputs.shape[0]
-    tokens, rank = probe.shape
-    tile = -(-features // 64) * 16
-    tiles = pl.cdiv(features, tile) // pieces
-    first = piece * tiles
+    shape = jax.ShapeDtypeStruct((plain + TERMS * exact, rank), jnp.bfloat16)
+    return order.call(kernel, (pair, arrived), shape, after)
+
+
+def pieces_of(chunks):
+    if not isinstance(chunks, list):
+        return [chunks], None
+    parts = [array for own, received, _ in chunks for array in (own, received)]
+
+    def fill(refs, probe):
+        place = lax.axis_index("owner")
+        inner = (place == 1) | (place == 2)
+        start = 0
+        for i, (_, _, rows) in enumerate(chunks):
+            own, received = refs[2 * i], refs[2 * i + 1]
+            probe[start : start + rows, :] = jnp.where(inner, own[:rows, :], received[:rows, :])
+            start += rows
+
+    return parts, fill
+
+
+def data_half(order, inputs, chunks, half, before):
+    features, tokens = inputs.shape
+    parts, fill = pieces_of(chunks)
+    rank = parts[0].shape[1]
+    quarter = features // 4
+    depth = tokens // SPLIT
+    shape = pltpu.HBM((2, quarter, rank), jnp.float32)
+    out_spec = pl.BlockSpec((1, quarter, rank), lambda i: (half, 0, 0))
 
     def kernel(x, p, *refs):
-        refs[-1][...] = jnp.dot(x[...], p[...], preferred_element_type=jnp.float32)
-
-    before = () if data is None else (data,)
+        given, kept, total = refs[-3:]
+        odd = lax.axis_index("context") % 2 == 1
+        step = pl.program_id(0)
+        product = jnp.dot(x[...], p[...], preferred_element_type=jnp.float32)
+
+        @pl.when(step == 0)
+        def _():
+            total[...] = product
+
+        @pl.when(step > 0)
+        def _():
+            total[...] += product
+
+        @pl.when((step == SPLIT - 1) & odd)
+        def _():
+            given[0] = total[:quarter, :]
+            kept[0] = total[quarter:, :]
+
+        @pl.when((step == SPLIT - 1) & jnp.logical_not(odd))
+        def _():
+            kept[0] = total[:quarter, :]
+            given[0] = total[quarter:, :]
+
     return order.call(
         kernel,
-        (inputs, probe, *before),
-        pltpu.HBM((features, rank), jnp.float32),
-        vmem=52 * MIB,
-        grid=(tiles,),
+        (inputs, *parts, *before),
+        (shape, shape),
+        vmem=ROOM * MIB,
+        grid=(SPLIT,),
         in_specs=[
-            pl.BlockSpec((tile, tokens), lambda i: (first + i, 0)),
-            pl.BlockSpec((tokens, rank), lambda i: (0, 0)),
+            pl.BlockSpec((2 * quarter, depth), lambda i: (half, i)),
+            pl.BlockSpec((depth, rank), lambda i: (i, 0)),
             *[ANYWHERE] * len(before),
         ],
-        out_specs=[pl.BlockSpec((tile, rank), lambda i: (first + i, 0))],
-        input_output_aliases={2: 0} if before else {},
-    )
-
-
-def data_parts(order, inputs, probe, after):
-    tokens, rank = probe.shape
+        out_specs=[out_spec, out_spec],
+        scratch_shapes=[pltpu.VMEM((2 * quarter, rank), jnp.float32)],
+        input_output_aliases={2: 0, 3: 1} if before else {},
+    )
+
+
+def data_parts(order, inputs, chunks, after):
+    tokens = inputs.shape[0]
+    parts, fill = pieces_of(chunks)
+    rank = parts[0].shape[1]
     quarter = inputs.shape[1] // 4
     shape = jax.ShapeDtypeStruct((2, quarter, rank), jnp.float32)
     out_spec = pl.BlockSpec((1, quarter, rank), lambda i: (i, 0, 0))
 
-    def kernel(x, p, given, kept):
+    def kernel(x, *refs):
+        given, kept, probe = refs[-3:] if fill else (*refs[-2:], refs[0])
+        if fill:
+            pl.when(pl.program_id(0) == 0)(lambda: fill(refs, probe))
         odd = lax.axis_index("context") % 2 == 1
-        product = token_contract(x[...], p[...])
+        product = token_contract(x[...], probe[...])
         given[0] = jnp.where(odd, product[:quarter], product[quarter:])
         kept[0] = jnp.where(odd, product[quarter:], product[:quarter])
 
     return order.call(
         kernel,
-        (inputs, probe),
+        (inputs, *parts),
         (shape, shape),
         after,
-        vmem=52 * MIB,
+        vmem=ROOM * MIB,
         grid=(2,),
         in_specs=[
             pl.BlockSpec((tokens, 2 * quarter), lambda i: (0, i)),
-            pl.BlockSpec((tokens, rank), lambda i: (0, 0)),
+            *[pl.BlockSpec(p.shape, lambda i: (0, 0)) for p in parts],
         ],
         out_specs=[out_spec, out_spec],
+        scratch_shapes=[pltpu.VMEM((tokens, rank), jnp.bfloat16)] if fill else [],
     )
 
 
@@ -291,7 +347,7 @@
         (kept, arrived),
         (shape, packed_shape(shape, rows)),
         scratch_shapes=[pltpu.VMEM((rows, rank), jnp.float32)],
-        vmem=12 * MIB,
+        vmem=(8 + rows // 96) * MIB,
     )
 
 
@@ -320,10 +376,10 @@
 
     shape = jax.ShapeDtypeStruct((rows, rank), jnp.float32)
     operands = (basis, eigen.reshape(1, rank), cores, *shares)
-    return order.call(kernel, operands, shape, vmem=16 * MIB)
-
-
-def core_parts(order, bases, omegas, after):
+    return order.call(kernel, operands, shape, vmem=24 * MIB)
+
+
+def core_parts(order, bases, omegas):
     rank = omegas[0].shape[1]
     share = rank // lax.axis_size("context")
     count = len(bases)
@@ -337,25 +393,26 @@
 
     shape = jax.ShapeDtypeStruct((count * share, rank), jnp.float32)
     scratch = [pltpu.VMEM((rank, rank), jnp.float32)]
-    return order.call(kernel, (*bases, *omegas), shape, after, 52 * MIB, scratch_shapes=scratch)
+    return order.call(kernel, (*bases, *omegas), shape, vmem=ROOM * MIB, scratch_shapes=scratch)
 
 
 def lines_of_four(inputs, omegas, bases, eigens, scale):
-    place = lax.axis_index("owner")
-    inner = (place == 1) | (place == 2)
     turned = [x.shape[1] % 128 != 0 for x in inputs]
-    inputs = [x.T if t else x for x, t in zip(inputs, turned)]
+    inputs = [
+        pltpu.with_memory_space_constraint(x.T if t else x, pltpu.HBM) if FENCED else x.T if t else x
+        for x, t in zip(inputs, turned)
+    ]
     order = Order()
     jobs = [k for k, _ in CHUNKS]
     count = len(jobs)
-    partial, plain, message, inward, pair, across, probe, outward, chunk = (
-        [None] * count for _ in range(9)
+    partial, plain, message, inward, pair, across, probe, outward = (
+        [None] * count for _ in range(8)
     )
     state = [None] * 3
     results = [None] * 3
     rank = omegas[0].shape[1]
 
-    def multiply(i):
+    def multiply(i, after=()):
         k, share = CHUNKS[i]
         unit = inputs[k].shape[1 if turned[k] else 0] // 16
         start = unit * sum(n for j, n in CHUNKS[:i] if j == k)
@@ -364,7 +421,7 @@
         if i == CARRIER:
             partial[i] = jnp.concatenate([partial[i], cores], 0)
         plain[i] = rows
-        message[i] = packed(order, partial[i], rows)
+        message[i] = packed(order, partial[i], rows, after)
 
     def send(i, after=()):
         if after:
@@ -375,32 +432,33 @@
         pair[i], sums = paired(order, partial[i], inward[i], plain[i])
         across[i] = lax.ppermute(sums, "owner", ACROSS)
 
-    def add_across(i):
-        probe[i] = rounded(order, pair[i], across[i], plain[i])
+    def add_across(i, after=()):
+        probe[i] = rounded(order, pair[i], across[i], plain[i], after)
         outward[i] = lax.ppermute(probe[i], "owner", OUTWARD)
 
     def carried(i):
-        whole = lax.select(inner, probe[i], outward[i])
-        if i != CARRIER:
-            return whole, None
-        terms = whole[plain[i] :].reshape(3, cores.shape[0], rank).astype(jnp.float32)
-        return whole[: plain[i]], terms[0] + (terms[1] + terms[2])
+        place = lax.axis_index("owner")
+        inner = (place == 1) | (place == 2)
+        terms = lax.select(inner, probe[i][plain[i] :], outward[i][plain[i] :])
+        return jnp.sum(terms.reshape(TERMS, cores.shape[0], rank).astype(jnp.float32), 0)
 
     def probes(k):
-        return jnp.concatenate([chunk[i] for i in range(count) if jobs[i] == k], 0)
+        mine = [i for i in range(count) if jobs[i] == k]
+        if not SELECTED:
+            return [(probe[i], outward[i], plain[i]) for i in mine]
+        place = lax.axis_index("owner")
+        inner = (place == 1) | (place == 2)
+        whole = [lax.select(inner, probe[i], outward[i])[: plain[i]] for i in mine]
+        return jnp.concatenate(whole, 0)
 
     def contract(k, after=()):
         given, kept = data_parts(order, inputs[k], probes(k), after)
         state[k] = kept, given
 
     def share_out(k, now=False):
-        if turned[k]:
-            data = order.gate(state[k], (), True)
-            state[k] = (lax.psum_scatter(data, "context", scatter_dimension=0, tiled=True),)
-        else:
-            kept, given = state[k]
-            given = given if now else order.gate(given)
-            state[k] = kept, lax.ppermute(given, "context", PAIRED)
+        kept, given = state[k]
+        given = given if now else order.gate(given, (), turned[k])
+        state[k] = kept, lax.ppermute(given, "context", PAIRED)
 
     def add_cores(k):
         stays, given = core_summed(order, *state[k])
@@ -408,10 +466,6 @@
 
     def finish(k):
         results[k] = finished(order, picked[k], eigens[k], whole, k, state[k], scale)
-
-    def receive(i):
-        chunk[i], total = carried(i)
-        return total
 
     def swapped(array, pairs, upper):
         theirs = lax.ppermute(order.gate(array), "context", pairs)
@@ -422,45 +476,51 @@
     context = lax.axis_index("context")
     quarters = [b.shape[0] // 4 for b in bases]
     picked = [lax.dynamic_slice_in_dim(b, context * n, n, 0) for b, n in zip(bases, quarters)]
+    halves = ()
     multiply(0)
     send(0)
     multiply(1)
     for i in range(count):
-        ahead = i + 1 < count
-        shrinks = ahead and message[i].shape[0] > message[i + 1].shape[0]
-        came = (inward[i],) if i < 2 else (inward[i], outward[i - 2])
-        if shrinks:
-            add_pair(i)
-        if ahead:
-            send(i + 1, came)
-        if not shrinks:
-            add_pair(i)
-        if i > 0:
-            add_across(i - 1)
-        if i == 4:
+        for act in STEPS[i]:
+            if act == "B":
+                add_pair(i)
+            elif act == "R":
+                add_across(i - 1)
+            else:
+                send(i + 1, (inward[i],) if i < 2 else (inward[i], outward[i - 2]))
+        if i == SWAPS[0]:
+            pairs = swapped(totals, PAIRED, context % 2 == 1)
+        if i == SWAPS[1]:
+            whole = swapped(pairs, SKIPPED, context >= 2)
+        if i == SHARED:
             share_out(2)
-            pairs = swapped(totals, PAIRED, context % 2 == 1)
+        if i == CARRIER - 2:
+            cores = core_parts(order, bases, omegas)
+        if i + 2 < count:
+            multiply(i + 2, picked if i == 0 else ())
+        if i in PIECES:
+            halves = data_half(order, inputs[2], probes(2), PIECES.index(i), halves)
+            state[2] = halves[1], halves[0]
+        if i == ATTN:
+            contract(0, (whole,) if WAITS == 2 else ())
+        if i == CARRIER + 1:
+            totals = carried(CARRIER)
         if i == 5:
-            whole = swapped(pairs, SKIPPED, context >= 2)
-        if i == CARRIER - 2:
-            cores = core_parts(order, bases, omegas, picked)
-        if i + 2 < count:
-            multiply(i + 2)
-        if i > 0:
-            got = receive(i - 1)
-            totals = got if i - 1 == CARRIER else totals if i > CARRIER + 1 else None
-        if i in (2, 3):
-            state[2] = data_rows(order, inputs[2], probes(2), i - 2, 2, state[2])
-        if i == 4:
-            contract(0)
+            share_out(0)
+        if i == SUMMED:
+            add_cores(2)
+        if i == 5:
+            add_cores(0)
     add_across(count - 1)
-    share_out(0)
-    add_cores(0)
-    receive(count - 1)
-    contract(1)
+    if EARLY == 1:
+        finish(2)
+    contract(1, (whole,) if WAITS == 1 else ())
     share_out(1, True)
+    if EARLY == 2:
+        finish(2)
     add_cores(1)
-    finish(2)
+    if EARLY == 0:
+        finish(2)
     finish(0)
     finish(1)
     return tuple(results)

time: 234 us -> 223 us (0.953)
  between operations: 14.6 us -> 1.48 us
  waiting for transfers between devices: 54.3 us -> 65.9 us
  Pallas kernels: 95.4 us -> 91.5 us
  starting transfers between devices: 49.2 us -> 45.5 us
  other arithmetic: 6.08 us -> 3.66 us
    ppermute x2 -> x3, waiting for transfers between devices: 8.04 us -> 15 us  [add_cores(): state[k] = (stays, lax.ppermute(given, 'context', SKIPPED))]
    ppermute x6, waiting for transfers between devices: 25.4 us -> 32.3 us  [add_across(): outward[i] = lax.ppermute(probe[i], 'owner', OUTWARD)]
    pallas_call x43 -> x44, Pallas kernels: 95.4 us -> 91.5 us  [call(): pl.pallas_call(body, out_shape=(*outs, jax.ShapeDtypeStruct((8, 128), jnp...]
    ppermute x2, waiting for transfers between devices: 4.62 us -> 1.44 us  [swapped(): theirs = lax.ppermute(order.gate(array), 'context', pairs)]
    ppermute x6, starting transfers between devices: 30.2 us -> 27.7 us  [send(): inward[i] = lax.ppermute(message[i], 'owner', INWARD)]
    unnamed x61 -> x70, local copies, waits for them, and re-layouts: 10.4 us -> 9.44 us
  transfers between devices with their start and end apart: 25 -> 26, of which waited for: 10 -> 11; matrix products, arithmetic and copies ran while one was open for 4% -> 2% of each run, Pallas kernels for 35% -> 36%
where the time goes in v3:
time: 223 us; the launch traced here: 220 us
  Pallas kernels  91.5 us (41%)
  waiting for transfers between devices  65.9 us (30%)
  starting transfers between devices  45.5 us (20%)
  local copies, waits for them, and re-layouts  11.7 us (5%)
  other arithmetic  3.66 us (2%)
    pallas_call x44, Pallas kernels, call(): pl.pallas_call(body, out_shape=(*outs, jax.ShapeDtypeStruct((8, 128), jnp...  91.5 us
    ppermute x6, waiting for transfers between devices, add_across(): outward[i] = lax.ppermute(probe[i], 'owner', OUTWARD)  32.3 us
    ppermute x6, starting transfers between devices, send(): inward[i] = lax.ppermute(message[i], 'owner', INWARD)  27.7 us
    ppermute x6, waiting for transfers between devices, send(): inward[i] = lax.ppermute(message[i], 'owner', INWARD)  17.1 us
    ppermute x3, waiting for transfers between devices, add_cores(): state[k] = (stays, lax.ppermute(given, 'context', SKIPPED))  15 us
    unnamed x70, local copies, waits for them, and re-layouts  9.44 us
    ppermute x6, starting transfers between devices, add_across(): outward[i] = lax.ppermute(probe[i], 'owner', OUTWARD)  8.3 us
    ppermute x6, starting transfers between devices, add_pair(): across[i] = lax.ppermute(sums, 'owner', ACROSS)  5.3 us
  transfers between devices with their start and end apart: 26, of which 11 were waited for; matrix products, arithmetic and copies ran while one was open for 2% of the time, Pallas kernels for 36%

profile of v3, /device:TPU:0, one launch (start us, length us, event | category | flops | bytes accessed | tf_op | source)
XLA Modules:
  0.0 219.7 jit_solution(9386853740394174346)
XLA Ops:
  0.6 8.6 %shard_map.139 = (f32[1024,256]{1,0:T(8,128)S(1)}, f32[8,128]{1,0:T(8,128)S(1)}) custom-call(bf16[7392,2048]{1,0:T(8,128)(2,1)} %bitcast.9, bf16[7392,256]{1,0:T(8,128)(2,1)} %refs_5_.1), custom_call_target="tpu_custom_call" | custom-call | flops 1000000000 | bytes 10000000 | tf_op jit(solution)/shard_map/pallas_call | solution.py:80
  9.6 5.0 %collective-permute-start = (f32[696,256]{1,0:T(8,128)S(1)}, f32[696,256]{1,0:T(8,128)S(1)}, u32[]{:S(2)}, u32[]{:S(2)}) collective-permute-start(f32[696,256]{1,0:T(8,128)S(1)} %get-tuple-element.105), channel_id=1, source_target_pairs={{0,4},{12,8},{1,5},{13,9},{2,6},{14,10},{3,7},{15,11},{16,20},{28,... | collective-permute-start | bytes 2138120 | tf_op jit(solution)/shard_map/ppermute | solution.py:429
  14.6 8.7 %shard_map.141 = (f32[1024,256]{1,0:T(8,128)S(1)}, f32[8,128]{1,0:T(8,128)S(1)}) custom-call(bf16[7392,2048]{1,0:T(8,128)(2,1)} %bitcast.10, bf16[7392,256]{1,0:T(8,128)(2,1)} %refs_5_.1, f32[8,128]{1,0:T(8,128)S(1)} %get-tuple-element.106.refs_2_), custom_call_target="tpu_custom_call" | custom-call | flops 1000000000 | bytes 10000000 | tf_op jit(solution)/shard_map/pallas_call | solution.py:80
  25.0 4.8 %collective-permute-done.refs_2_.refs_1_ = f32[696,256]{1,0:T(8,128)S(1)} collective-permute-done((f32[696,256]{1,0:T(8,128)S(1)}, f32[696,256]{1,0:T(8,128)S(1)}, u32[]{:S(2)}, u32[]{:S(2)}) %collective-permute-start) | collective-permute-done | bytes 712736 | tf_op jit(solution)/shard_map/ppermute | solution.py:429
  29.8 4.4 %collective-permute-start.1 = (f32[696,256]{1,0:T(8,128)S(1)}, f32[696,256]{1,0:T(8,128)S(1)}, u32[]{:S(2)}, u32[]{:S(2)}) collective-permute-start(f32[696,256]{1,0:T(8,128)S(1)} %get-tuple-element.119), channel_id=1, source_target_pairs={{0,4},{12,8},{1,5},{13,9},{2,6},{14,10},{3,7},{15,11},{16,20},{28,... | collective-permute-start | bytes 2138120 | tf_op jit(solution)/shard_map/ppermute | solution.py:429
  36.7 6.0 %shard_map.145 = (f32[192,256]{1,0:T(8,128)S(1)}, f32[8,128]{1,0:T(8,128)S(1)}) custom-call(bf16[2048,256]{1,0:T(8,128)(2,1)S(1)} %copy-done.1, bf16[2048,256]{1,0:T(8,128)(2,1)} %refs_1_.9, bf16[7392,256]{1,0:T(8,128)(2,1)} %refs_2_.1, bf16[2048,256]{1,0:T(8,128)(2,1)} %refs_1_.11, bf16[2048,256]{1,0:T(8,128)(2,1)} %refs_1_.13, bf16[7392,256]{1,0:T(8,128)(2,1)} %refs_5_.1, ...), custom_call_target="tpu_custom_call" | custom-call | flops 1000000000 | bytes 10000000 | tf_op jit(solution)/shard_map/pallas_call | solution.py:80
  42.7 3.3 %shard_map.146 = (f32[1024,256]{1,0:T(8,128)S(1)}, f32[8,128]{1,0:T(8,128)S(1)}) custom-call(bf16[2048,2048]{1,0:T(8,128)(2,1)} %refs_0_.12, bf16[2048,256]{1,0:T(8,128)(2,1)} %refs_1_.11, f32[8,128]{1,0:T(8,128)S(1)} %get-tuple-element.113.refs_2_), custom_call_target="tpu_custom_call" | custom-call | flops 1000000000 | bytes 10000000 | tf_op jit(solution)/shard_map/pallas_call | solution.py:80
  48.5 4.4 %collective-permute-start.2 = (f32[888,256]{1,0:T(8,128)S(1)}, f32[888,256]{1,0:T(8,128)S(1)}, u32[]{:S(2)}, u32[]{:S(2)}) collective-permute-start(f32[888,256]{1,0:T(8,128)S(1)} %get-tuple-element.120), channel_id=1, source_target_pairs={{0,4},{12,8},{1,5},{13,9},{2,6},{14,10},{3,7},{15,11},{16,20},{28,... | collective-permute-start | bytes 2727944 | tf_op jit(solution)/shard_map/ppermute | solution.py:429
  56.4 3.3 %shard_map.151 = (f32[1024,256]{1,0:T(8,128)S(1)}, f32[8,128]{1,0:T(8,128)S(1)}) custom-call(bf16[2048,2048]{1,0:T(8,128)(2,1)} %refs_0_.12, bf16[2048,256]{1,0:T(8,128)(2,1)} %refs_1_.11, f32[8,128]{1,0:T(8,128)S(1)} %get-tuple-element.125.refs_2_), custom_call_target="tpu_custom_call" | custom-call | flops 1000000000 | bytes 10000000 | tf_op jit(solution)/shard_map/pallas_call | solution.py:80
  60.2 10.3 %collective-permute-done.2.refs_1_.refs_2_ = f32[888,256]{1,0:T(8,128)S(1)} collective-permute-done((f32[888,256]{1,0:T(8,128)S(1)}, f32[888,256]{1,0:T(8,128)S(1)}, u32[]{:S(2)}, u32[]{:S(2)}) %collective-permute-start.2) | collective-permute-done | bytes 909344 | tf_op jit(solution)/shard_map/ppermute | solution.py:429
  76.1 4.6 %collective-permute-start.6 = (f32[696,256]{1,0:T(8,128)}, f32[696,256]{1,0:T(8,128)S(1)}, u32[]{:S(2)}, u32[]{:S(2)}) collective-permute-start(f32[696,256]{1,0:T(8,128)} %copy-done.18), channel_id=1, source_target_pairs={{0,4},{12,8},{1,5},{13,9},{2,6},{14,10},{3,7},{15,11},{16,20},{28,... | collective-permute-start | bytes 2138120 | tf_op jit(solution)/shard_map/ppermute | solution.py:429
  87.8 10.2 %shard_map.158 = (f32[2,1848,256]{2,1,0:T(8,128)}, f32[2,1848,256]{2,1,0:T(8,128)}, f32[8,128]{1,0:T(8,128)S(1)}) custom-call(bf16[7392,2048]{1,0:T(8,128)(2,1)} %bitcast.11, bf16[2048,256]{1,0:T(8,128)(2,1)S(1)} %pad_maximum_fusion.refs_1_, f32[8,128]{1,0:T(8,128)S(1)} %get-tuple-element.143.refs_2_), custom_call_target="tpu_custom_call" | custom-call | flops 1000000000 | bytes 10000000 | tf_op jit(solution)/shard_map/pallas_call | solution.py:80
  101.9 4.6 %collective-permute-start.11 = (f32[696,256]{1,0:T(8,128)S(1)}, f32[696,256]{1,0:T(8,128)S(1)}, u32[]{:S(2)}, u32[]{:S(2)}) collective-permute-start(f32[696,256]{1,0:T(8,128)S(1)} %get-tuple-element.150), channel_id=1, source_target_pairs={{0,4},{12,8},{1,5},{13,9},{2,6},{14,10},{3,7},{15,11},{16,20},{28,... | collective-permute-start | bytes 2138120 | tf_op jit(solution)/shard_map/ppermute | solution.py:429
  107.5 3.3 %shard_map.162 = (f32[1024,256]{1,0:T(8,128)S(1)}, f32[8,128]{1,0:T(8,128)S(1)}) custom-call(bf16[2048,2048]{1,0:T(8,128)(2,1)} %refs_0_.13, bf16[2048,256]{1,0:T(8,128)(2,1)} %refs_1_.13, f32[8,128]{1,0:T(8,128)S(1)} %get-tuple-element.151.refs_2_), custom_call_target="tpu_custom_call" | custom-call | flops 1000000000 | bytes 10000000 | tf_op jit(solution)/shard_map/pallas_call | solution.py:80
  111.2 10.2 %shard_map.164 = (f32[2,1848,256]{2,1,0:T(8,128)}, f32[2,1848,256]{2,1,0:T(8,128)}, f32[8,128]{1,0:T(8,128)S(1)}) custom-call(bf16[7392,2048]{1,0:T(8,128)(2,1)} %bitcast.12, bf16[2048,256]{1,0:T(8,128)(2,1)S(1)} %pad_maximum_fusion.refs_1_, f32[2,1848,256]{2,1,0:T(8,128)} %get-tuple-element.155.refs_2_, ...), custom_call_target="tpu_custom_call", output_to_operand_aliasing={{0}: (2, {}), {1}: (3, {})} | custom-call | flops 1000000000 | bytes 10000000 | tf_op jit(solution)/shard_map/pallas_call | solution.py:80
  129.5 4.6 %collective-permute-start.16 = (f32[696,256]{1,0:T(8,128)S(1)}, f32[696,256]{1,0:T(8,128)S(1)}, u32[]{:S(2)}, u32[]{:S(2)}) collective-permute-start(f32[696,256]{1,0:T(8,128)S(1)} %copy-done.17), channel_id=1, source_target_pairs={{0,4},{12,8},{1,5},{13,9},{2,6},{14,10},{3,7},{15,11},{16,20},{28,... | collective-permute-start | bytes 2138120 | tf_op jit(solution)/shard_map/ppermute | solution.py:429
  134.9 9.4 %collective-permute-done.14 = bf16[1024,256]{1,0:T(8,128)(2,1)S(1)} collective-permute-done((bf16[1024,256]{1,0:T(8,128)(2,1)S(1)}, bf16[1024,256]{1,0:T(8,128)(2,1)S(1)}, u32[]{:S(2)}, u32[]{:S(2)}) %collective-permute-start.14) | collective-permute-done | bytes 524320 | tf_op jit(solution)/shard_map/ppermute | solution.py:437
  145.4 6.3 %shard_map.171 = (f32[2,512,256]{2,1,0:T(8,128)}, f32[2,512,256]{2,1,0:T(8,128)}, f32[8,128]{1,0:T(8,128)S(1)}) custom-call(bf16[2048,2048]{1,0:T(8,128)(2,1)} %refs_0_.12, bf16[2048,256]{1,0:T(8,128)(2,1)} %pad_maximum_fusion.1.refs_1_, f32[8,128]{1,0:T(8,128)S(1)} %get-tuple-element.168.refs_2_), custom_call_target="tpu_custom_call" | custom-call | flops 1000000000 | bytes 10000000 | tf_op jit(solution)/shard_map/pallas_call | solution.py:80
  168.7 4.5 %collective-permute-done.20 = bf16[1024,256]{1,0:T(8,128)(2,1)S(1)} collective-permute-done((bf16[1024,256]{1,0:T(8,128)(2,1)S(1)}, bf16[1024,256]{1,0:T(8,128)(2,1)S(1)}, u32[]{:S(2)}, u32[]{:S(2)}) %collective-permute-start.20) | collective-permute-done | bytes 524320 | tf_op jit(solution)/shard_map/ppermute | solution.py:437
  173.9 15.9 %collective-permute-done.22 = bf16[1024,256]{1,0:T(8,128)(2,1)S(1)} collective-permute-done((bf16[1024,256]{1,0:T(8,128)(2,1)S(1)}, bf16[1024,256]{1,0:T(8,128)(2,1)S(1)}, u32[]{:S(2)}, u32[]{:S(2)}) %collective-permute-start.22) | collective-permute-done | bytes 524320 | tf_op jit(solution)/shard_map/ppermute | solution.py:437
  190.9 6.0 %shard_map.178 = (f32[2,512,256]{2,1,0:T(8,128)S(1)}, f32[2,512,256]{2,1,0:T(8,128)}, f32[8,128]{1,0:T(8,128)S(1)}) custom-call(bf16[2048,2048]{1,0:T(8,128)(2,1)} %refs_0_.13, bf16[2048,256]{1,0:T(8,128)(2,1)} %pad_maximum_fusion.2.refs_1_, f32[8,128]{1,0:T(8,128)S(1)} %get-tuple-element.189.refs_2_, f32[768,256]{1,0:T(8,128)S(1)} %pad_maximum_fusion.3.refs_3_.refs_2_), custom_call_target="tpu_custom_call" | custom-call | flops 1000000000 | bytes 10000000 | tf_op jit(solution)/shard_map/pallas_call | solution.py:80
  198.5 5.7 %collective-permute-done.24.refs_4_ = f32[1240,256]{1,0:T(8,128)S(1)} collective-permute-done((f32[1240,256]{1,0:T(8,128)S(1)}, f32[1240,256]{1,0:T(8,128)S(1)}, u32[]{:S(2)}, u32[]{:S(2)}) %collective-permute-start.24) | collective-permute-done | bytes 1269792 | tf_op jit(solution)/shard_map/ppermute | solution.py:465
  207.8 4.4 %collective-permute-done.19.refs_4_ = f32[360,256]{1,0:T(8,128)S(1)} collective-permute-done((f32[360,256]{1,0:T(8,128)S(1)}, f32[360,256]{1,0:T(8,128)S(1)}, u32[]{:S(2)}, u32[]{:S(2)}) %collective-permute-start.19) | collective-permute-done | bytes 368672 | tf_op jit(solution)/shard_map/ppermute | solution.py:465
  213.5 4.9 %collective-permute-done.25.refs_4_ = f32[360,256]{1,0:T(8,128)S(1)} collective-permute-done((f32[360,256]{1,0:T(8,128)S(1)}, f32[360,256]{1,0:T(8,128)S(1)}, u32[]{:S(2)}, u32[]{:S(2)}) %collective-permute-start.25) | collective-permute-done | bytes 368672 | tf_op jit(solution)/shard_map/ppermute | solution.py:465
  (160 shorter events, 64.6 us)
Async XLA Ops:
  9.6 20.1 %collective-permute-start = (f32[696,256]{1,0:T(8,128)S(1)}, f32[696,256]{1,0:T(8,128)S(1)}, u32[]{:S(2)}, u32[]{:S(2)}) collective-permute-start(f32[696,256]{1,0:T(8,128)S(1)} %get-tuple-element.105), channel_id=1, source_target_pairs={{0,4},{12,8},{1,5},{13,9},{2,6},{14,10},{3,7},{15,11},{16,20},{28,... | collective-permute-start | bytes 2138120 | tf_op jit(solution)/shard_map/ppermute | solution.py:429
  29.8 18.7 %collective-permute-start.1 = (f32[696,256]{1,0:T(8,128)S(1)}, f32[696,256]{1,0:T(8,128)S(1)}, u32[]{:S(2)}, u32[]{:S(2)}) collective-permute-start(f32[696,256]{1,0:T(8,128)S(1)} %get-tuple-element.119), channel_id=1, source_target_pairs={{0,4},{12,8},{1,5},{13,9},{2,6},{14,10},{3,7},{15,11},{16,20},{28,... | collective-permute-start | bytes 2138120 | tf_op jit(solution)/shard_map/ppermute | solution.py:429
  36.0 18.4 %collective-permute-start.3 = (f32[696,256]{1,0:T(8,128)S(1)}, f32[696,256]{1,0:T(8,128)S(1)}, u32[]{:S(2)}, u32[]{:S(2)}) collective-permute-start(f32[696,256]{1,0:T(8,128)S(1)} %get-tuple-element.122), channel_id=1, source_target_pairs={{4,8},{8,4},{5,9},{9,5},{6,10},{10,6},{7,11},{11,7},{20,24},{24,20... | collective-permute-start | bytes 2138120 | tf_op jit(solution)/shard_map/ppermute | solution.py:433
  48.5 22.0 %collective-permute-start.2 = (f32[888,256]{1,0:T(8,128)S(1)}, f32[888,256]{1,0:T(8,128)S(1)}, u32[]{:S(2)}, u32[]{:S(2)}) collective-permute-start(f32[888,256]{1,0:T(8,128)S(1)} %get-tuple-element.120), channel_id=1, source_target_pairs={{0,4},{12,8},{1,5},{13,9},{2,6},{14,10},{3,7},{15,11},{16,20},{28,... | collective-permute-start | bytes 2727944 | tf_op jit(solution)/shard_map/ppermute | solution.py:429
  53.7 18.6 %collective-permute-start.7 = (f32[696,256]{1,0:T(8,128)S(1)}, f32[696,256]{1,0:T(8,128)S(1)}, u32[]{:S(2)}, u32[]{:S(2)}) collective-permute-start(f32[696,256]{1,0:T(8,128)S(1)} %get-tuple-element.136), channel_id=1, source_target_pairs={{4,8},{8,4},{5,9},{9,5},{6,10},{10,6},{7,11},{11,7},{20,24},{24,20... | collective-permute-start | bytes 2138120 | tf_op jit(solution)/shard_map/ppermute | solution.py:433
  55.0 17.4 %collective-permute-start.5 = (bf16[1024,256]{1,0:T(8,128)(2,1)S(1)}, bf16[1024,256]{1,0:T(8,128)(2,1)S(1)}, u32[]{:S(2)}, u32[]{:S(2)}) collective-permute-start(bf16[1024,256]{1,0:T(8,128)(2,1)S(1)} %get-tuple-element.133), channel_id=1, source_target_pairs={{4,0},{8,12},{5,1},{9,13},{6,2},{10,14},{7,3},{11,15},{20,16},{24,... | collective-permute-start | bytes 1572872 | tf_op jit(solution)/shard_map/ppermute | solution.py:437
  74.7 13.0 %collective-permute-start.8 = (bf16[1024,256]{1,0:T(8,128)(2,1)S(1)}, bf16[1024,256]{1,0:T(8,128)(2,1)S(1)}, u32[]{:S(2)}, u32[]{:S(2)}) collective-permute-start(bf16[1024,256]{1,0:T(8,128)(2,1)S(1)} %get-tuple-element.142), channel_id=1, source_target_pairs={{4,0},{8,12},{5,1},{9,13},{6,2},{10,14},{7,3},{11,15},{20,16},{24,... | collective-permute-start | bytes 1572872 | tf_op jit(solution)/shard_map/ppermute | solution.py:437
  76.1 21.9 %collective-permute-start.6 = (f32[696,256]{1,0:T(8,128)}, f32[696,256]{1,0:T(8,128)S(1)}, u32[]{:S(2)}, u32[]{:S(2)}) collective-permute-start(f32[696,256]{1,0:T(8,128)} %copy-done.18), channel_id=1, source_target_pairs={{0,4},{12,8},{1,5},{13,9},{2,6},{14,10},{3,7},{15,11},{16,20},{28,... | collective-permute-start | bytes 2138120 | tf_op jit(solution)/shard_map/ppermute | solution.py:429
  80.7 19.3 %collective-permute-start.4 = (f32[888,256]{1,0:T(8,128)}, f32[888,256]{1,0:T(8,128)S(1)}, u32[]{:S(2)}, u32[]{:S(2)}) collective-permute-start(f32[888,256]{1,0:T(8,128)} %copy-done.13), channel_id=1, source_target_pairs={{4,8},{8,4},{5,9},{9,5},{6,10},{10,6},{7,11},{11,7},{20,24},{24,20... | collective-permute-start | bytes 2727944 | tf_op jit(solution)/shard_map/ppermute | solution.py:433
  100.6 20.8 %collective-permute-start.9 = (bf16[1600,256]{1,0:T(8,128)(2,1)S(1)}, bf16[1600,256]{1,0:T(8,128)(2,1)S(1)}, u32[]{:S(2)}, u32[]{:S(2)}) collective-permute-start(bf16[1600,256]{1,0:T(8,128)(2,1)S(1)} %get-tuple-element.147), channel_id=1, source_target_pairs={{4,0},{8,12},{5,1},{9,13},{6,2},{10,14},{7,3},{11,15},{20,16},{24,... | collective-permute-start | bytes 2457608 | tf_op jit(solution)/shard_map/ppermute | solution.py:437
  101.9 19.6 %collective-permute-start.11 = (f32[696,256]{1,0:T(8,128)S(1)}, f32[696,256]{1,0:T(8,128)S(1)}, u32[]{:S(2)}, u32[]{:S(2)}) collective-permute-start(f32[696,256]{1,0:T(8,128)S(1)} %get-tuple-element.150), channel_id=1, source_target_pairs={{0,4},{12,8},{1,5},{13,9},{2,6},{14,10},{3,7},{15,11},{16,20},{28,... | collective-permute-start | bytes 2138120 | tf_op jit(solution)/shard_map/ppermute | solution.py:429
  106.5 17.4 %collective-permute-start.10 = (f32[696,256]{1,0:T(8,128)S(1)}, f32[696,256]{1,0:T(8,128)S(1)}, u32[]{:S(2)}, u32[]{:S(2)}) collective-permute-start(f32[696,256]{1,0:T(8,128)S(1)} %get-tuple-element.149), channel_id=1, source_target_pairs={{4,8},{8,4},{5,9},{9,5},{6,10},{10,6},{7,11},{11,7},{20,24},{24,20... | collective-permute-start | bytes 2138120 | tf_op jit(solution)/shard_map/ppermute | solution.py:433
  127.9 30.7 %collective-permute-start.18 = (f32[2,1848,256]{2,1,0:T(8,128)}, f32[2,1848,256]{2,1,0:T(8,128)}, u32[]{:S(2)}, u32[]{:S(2)}) collective-permute-start(f32[2,1848,256]{2,1,0:T(8,128)} %get-tuple-element.179), channel_id=1, source_target_pairs={{0,1},{1,0},{2,3},{3,2},{4,5},{5,4},{6,7},{7,6},{8,9},{9,8},{10,11... | collective-permute-start | bytes 11354120 | tf_op jit(solution)/shard_map/ppermute | solution.py:461
  128.0 16.2 %collective-permute-start.14 = (bf16[1024,256]{1,0:T(8,128)(2,1)S(1)}, bf16[1024,256]{1,0:T(8,128)(2,1)S(1)}, u32[]{:S(2)}, u32[]{:S(2)}) collective-permute-start(bf16[1024,256]{1,0:T(8,128)(2,1)S(1)} %get-tuple-element.165), channel_id=1, source_target_pairs={{4,0},{8,12},{5,1},{9,13},{6,2},{10,14},{7,3},{11,15},{20,16},{24,... | collective-permute-start | bytes 1572872 | tf_op jit(solution)/shard_map/ppermute | solution.py:437
  129.5 22.2 %collective-permute-start.16 = (f32[696,256]{1,0:T(8,128)S(1)}, f32[696,256]{1,0:T(8,128)S(1)}, u32[]{:S(2)}, u32[]{:S(2)}) collective-permute-start(f32[696,256]{1,0:T(8,128)S(1)} %copy-done.17), channel_id=1, source_target_pairs={{0,4},{12,8},{1,5},{13,9},{2,6},{14,10},{3,7},{15,11},{16,20},{28,... | collective-permute-start | bytes 2138120 | tf_op jit(solution)/shard_map/ppermute | solution.py:429
  134.1 19.2 %collective-permute-start.15 = (f32[696,256]{1,0:T(8,128)S(1)}, f32[696,256]{1,0:T(8,128)S(1)}, u32[]{:S(2)}, u32[]{:S(2)}) collective-permute-start(f32[696,256]{1,0:T(8,128)S(1)} %copy-done.15), channel_id=1, source_target_pairs={{4,8},{8,4},{5,9},{9,5},{6,10},{10,6},{7,11},{11,7},{20,24},{24,20... | collective-permute-start | bytes 2138120 | tf_op jit(solution)/shard_map/ppermute | solution.py:433
  154.3 11.1 %collective-permute-start.21 = (f32[696,256]{1,0:T(8,128)}, f32[696,256]{1,0:T(8,128)}, u32[]{:S(2)}, u32[]{:S(2)}) collective-permute-start(f32[696,256]{1,0:T(8,128)} %get-tuple-element.186), channel_id=1, source_target_pairs={{4,8},{8,4},{5,9},{9,5},{6,10},{10,6},{7,11},{11,7},{20,24},{24,20... | collective-permute-start | bytes 2138120 | tf_op jit(solution)/shard_map/ppermute | solution.py:433
  155.8 12.8 %collective-permute-start.13 = (f32[384,256]{1,0:T(8,128)S(1)}, f32[384,256]{1,0:T(8,128)S(1)}, u32[]{:S(2)}, u32[]{:S(2)}) collective-permute-start(f32[384,256]{1,0:T(8,128)S(1)} %get-tuple-element.164), channel_id=1, source_target_pairs={{0,2},{2,0},{1,3},{3,1},{4,6},{6,4},{5,7},{7,5},{8,10},{10,8},{9,1... | collective-permute-start | bytes 1179656 | tf_op jit(solution)/shard_map/ppermute | solution.py:471
  157.3 15.9 %collective-permute-start.20 = (bf16[1024,256]{1,0:T(8,128)(2,1)S(1)}, bf16[1024,256]{1,0:T(8,128)(2,1)S(1)}, u32[]{:S(2)}, u32[]{:S(2)}) collective-permute-start(bf16[1024,256]{1,0:T(8,128)(2,1)S(1)} %get-tuple-element.184), channel_id=1, source_target_pairs={{4,0},{8,12},{5,1},{9,13},{6,2},{10,14},{7,3},{11,15},{20,16},{24,... | collective-permute-start | bytes 1572872 | tf_op jit(solution)/shard_map/ppermute | solution.py:437
  167.0 22.8 %collective-permute-start.22 = (bf16[1024,256]{1,0:T(8,128)(2,1)S(1)}, bf16[1024,256]{1,0:T(8,128)(2,1)S(1)}, u32[]{:S(2)}, u32[]{:S(2)}) collective-permute-start(bf16[1024,256]{1,0:T(8,128)(2,1)S(1)} %get-tuple-element.188), channel_id=1, source_target_pairs={{4,0},{8,12},{5,1},{9,13},{6,2},{10,14},{7,3},{11,15},{20,16},{24,... | collective-permute-start | bytes 1572872 | tf_op jit(solution)/shard_map/ppermute | solution.py:437
  173.3 30.9 %collective-permute-start.24 = (f32[1240,256]{1,0:T(8,128)S(1)}, f32[1240,256]{1,0:T(8,128)S(1)}, u32[]{:S(2)}, u32[]{:S(2)}) collective-permute-start(f32[1240,256]{1,0:T(8,128)S(1)} %get-tuple-element.193), channel_id=1, source_target_pairs={{0,2},{2,0},{1,3},{3,1},{4,6},{6,4},{5,7},{7,5},{8,10},{10,8},{9,1... | collective-permute-start | bytes 3809288 | tf_op jit(solution)/shard_map/ppermute | solution.py:465
  197.0 10.0 %collective-permute-start.23 = (f32[2,512,256]{2,1,0:T(8,128)S(1)}, f32[2,512,256]{2,1,0:T(8,128)S(1)}, u32[]{:S(2)}, u32[]{:S(2)}) collective-permute-start(f32[2,512,256]{2,1,0:T(8,128)S(1)} %get-tuple-element.191), channel_id=1, source_target_pairs={{0,1},{1,0},{2,3},{3,2},{4,5},{5,4},{6,7},{7,6},{8,9},{9,8},{10,11... | collective-permute-start | bytes 3145736 | tf_op jit(solution)/shard_map/ppermute | solution.py:461
  197.0 15.2 %collective-permute-start.19 = (f32[360,256]{1,0:T(8,128)S(1)}, f32[360,256]{1,0:T(8,128)S(1)}, u32[]{:S(2)}, u32[]{:S(2)}) collective-permute-start(f32[360,256]{1,0:T(8,128)S(1)} %get-tuple-element.183), channel_id=1, source_target_pairs={{0,2},{2,0},{1,3},{3,1},{4,6},{6,4},{5,7},{7,5},{8,10},{10,8},{9,1... | collective-permute-start | bytes 1105928 | tf_op jit(solution)/shard_map/ppermute | solution.py:465
  207.4 11.0 %collective-permute-start.25 = (f32[360,256]{1,0:T(8,128)S(1)}, f32[360,256]{1,0:T(8,128)S(1)}, u32[]{:S(2)}, u32[]{:S(2)}) collective-permute-start(f32[360,256]{1,0:T(8,128)S(1)} %get-tuple-element.199), channel_id=1, source_target_pairs={{0,2},{2,0},{1,3},{3,1},{4,6},{6,4},{5,7},{7,5},{8,10},{10,8},{9,1... | collective-permute-start | bytes 1105928 | tf_op jit(solution)/shard_map/ppermute | solution.py:465
  (36 other events, 162.2 us)

commit v4 on v3

--- a/solution.py
+++ b/solution.py
@@ -14,7 +14,7 @@
 SKIPPED = ((0, 2), (2, 0), (1, 3), (3, 1))
 CHUNKS = ((2, 8), (2, 8), (0, 8), (0, 8), (1, 8), (1, 8))
 CARRIER = 2
-TERMS = 3
+TERMS = 2
 STEPS = ("GB", "GBR", "BGR", "GBR", "GBR", "BR")
 SWAPS, SHARED, ATTN, PIECES = (4, 4), 4, 4, (2, 3)
 WAITS = 1

time: 223 us -> 220 us (0.987)
    unnamed x70 -> x68, local copies, waits for them, and re-layouts: 9.44 us -> 8.82 us
where the time goes in v4:
time: 220 us; the launch traced here: 217 us
  Pallas kernels  90.7 us (41%)
  waiting for transfers between devices  65.7 us (30%)
  starting transfers between devices  45.7 us (21%)
  local copies, waits for them, and re-layouts  11.1 us (5%)
  other arithmetic  2.74 us (1%)
    pallas_call x44, Pallas kernels, call(): pl.pallas_call(body, out_shape=(*outs, jax.ShapeDtypeStruct((8, 128), jnp...  90.7 us
    ppermute x6, waiting for transfers between devices, add_across(): outward[i] = lax.ppermute(probe[i], 'owner', OUTWARD)  32.2 us
    ppermute x6, starting transfers between devices, send(): inward[i] = lax.ppermute(message[i], 'owner', INWARD)  27.7 us
    ppermute x6, waiting for transfers between devices, send(): inward[i] = lax.ppermute(message[i], 'owner', INWARD)  17.1 us
    ppermute x3, waiting for transfers between devices, add_cores(): state[k] = (stays, lax.ppermute(given, 'context', SKIPPED))  15 us
    unnamed x68, local copies, waits for them, and re-layouts  8.82 us
    ppermute x6, starting transfers between devices, add_across(): outward[i] = lax.ppermute(probe[i], 'owner', OUTWARD)  8.3 us
    ppermute x6, starting transfers between devices, add_pair(): across[i] = lax.ppermute(sums, 'owner', ACROSS)  5.31 us
  transfers between devices with their start and end apart: 26, of which 11 were waited for; matrix products, arithmetic and copies ran while one was open for 2% of the time, Pallas kernels for 36%

profile of v4, /device:TPU:0, one launch (start us, length us, event | category | flops | bytes accessed | tf_op | source)
XLA Modules:
  0.0 217.4 jit_solution(10387744760824501217)
XLA Ops:
  0.6 8.6 %shard_map.139 = (f32[1024,256]{1,0:T(8,128)S(1)}, f32[8,128]{1,0:T(8,128)S(1)}) custom-call(bf16[7392,2048]{1,0:T(8,128)(2,1)} %bitcast.9, bf16[7392,256]{1,0:T(8,128)(2,1)} %refs_5_.1), custom_call_target="tpu_custom_call" | custom-call | flops 1000000000 | bytes 10000000 | tf_op jit(solution)/shard_map/pallas_call | solution.py:80
  9.6 5.0 %collective-permute-start = (f32[696,256]{1,0:T(8,128)S(1)}, f32[696,256]{1,0:T(8,128)S(1)}, u32[]{:S(2)}, u32[]{:S(2)}) collective-permute-start(f32[696,256]{1,0:T(8,128)S(1)} %get-tuple-element.105), channel_id=1, source_target_pairs={{0,4},{12,8},{1,5},{13,9},{2,6},{14,10},{3,7},{15,11},{16,20},{28,... | collective-permute-start | bytes 2138120 | tf_op jit(solution)/shard_map/ppermute | solution.py:429
  14.6 8.7 %shard_map.141 = (f32[1024,256]{1,0:T(8,128)S(1)}, f32[8,128]{1,0:T(8,128)S(1)}) custom-call(bf16[7392,2048]{1,0:T(8,128)(2,1)} %bitcast.10, bf16[7392,256]{1,0:T(8,128)(2,1)} %refs_5_.1, f32[8,128]{1,0:T(8,128)S(1)} %get-tuple-element.106.refs_2_), custom_call_target="tpu_custom_call" | custom-call | flops 1000000000 | bytes 10000000 | tf_op jit(solution)/shard_map/pallas_call | solution.py:80
  25.0 4.8 %collective-permute-done.refs_2_.refs_1_ = f32[696,256]{1,0:T(8,128)S(1)} collective-permute-done((f32[696,256]{1,0:T(8,128)S(1)}, f32[696,256]{1,0:T(8,128)S(1)}, u32[]{:S(2)}, u32[]{:S(2)}) %collective-permute-start) | collective-permute-done | bytes 712736 | tf_op jit(solution)/shard_map/ppermute | solution.py:429
  29.8 4.4 %collective-permute-start.1 = (f32[696,256]{1,0:T(8,128)S(1)}, f32[696,256]{1,0:T(8,128)S(1)}, u32[]{:S(2)}, u32[]{:S(2)}) collective-permute-start(f32[696,256]{1,0:T(8,128)S(1)} %get-tuple-element.119), channel_id=1, source_target_pairs={{0,4},{12,8},{1,5},{13,9},{2,6},{14,10},{3,7},{15,11},{16,20},{28,... | collective-permute-start | bytes 2138120 | tf_op jit(solution)/shard_map/ppermute | solution.py:429
  36.7 6.0 %shard_map.145 = (f32[192,256]{1,0:T(8,128)S(1)}, f32[8,128]{1,0:T(8,128)S(1)}) custom-call(bf16[2048,256]{1,0:T(8,128)(2,1)S(1)} %copy-done.1, bf16[2048,256]{1,0:T(8,128)(2,1)} %refs_1_.9, bf16[7392,256]{1,0:T(8,128)(2,1)} %refs_2_.1, bf16[2048,256]{1,0:T(8,128)(2,1)} %refs_1_.11, bf16[2048,256]{1,0:T(8,128)(2,1)} %refs_1_.13, bf16[7392,256]{1,0:T(8,128)(2,1)} %refs_5_.1, ...), custom_call_target="tpu_custom_call" | custom-call | flops 1000000000 | bytes 10000000 | tf_op jit(solution)/shard_map/pallas_call | solution.py:80
  42.7 3.3 %shard_map.146 = (f32[1024,256]{1,0:T(8,128)S(1)}, f32[8,128]{1,0:T(8,128)S(1)}) custom-call(bf16[2048,2048]{1,0:T(8,128)(2,1)} %refs_0_.12, bf16[2048,256]{1,0:T(8,128)(2,1)} %refs_1_.11, f32[8,128]{1,0:T(8,128)S(1)} %get-tuple-element.113.refs_2_), custom_call_target="tpu_custom_call" | custom-call | flops 1000000000 | bytes 10000000 | tf_op jit(solution)/shard_map/pallas_call | solution.py:80
  48.5 4.4 %collective-permute-start.2 = (f32[888,256]{1,0:T(8,128)S(1)}, f32[888,256]{1,0:T(8,128)S(1)}, u32[]{:S(2)}, u32[]{:S(2)}) collective-permute-start(f32[888,256]{1,0:T(8,128)S(1)} %get-tuple-element.120), channel_id=1, source_target_pairs={{0,4},{12,8},{1,5},{13,9},{2,6},{14,10},{3,7},{15,11},{16,20},{28,... | collective-permute-start | bytes 2727944 | tf_op jit(solution)/shard_map/ppermute | solution.py:429
  56.4 3.3 %shard_map.151 = (f32[1024,256]{1,0:T(8,128)S(1)}, f32[8,128]{1,0:T(8,128)S(1)}) custom-call(bf16[2048,2048]{1,0:T(8,128)(2,1)} %refs_0_.12, bf16[2048,256]{1,0:T(8,128)(2,1)} %refs_1_.11, f32[8,128]{1,0:T(8,128)S(1)} %get-tuple-element.125.refs_2_), custom_call_target="tpu_custom_call" | custom-call | flops 1000000000 | bytes 10000000 | tf_op jit(solution)/shard_map/pallas_call | solution.py:80
  60.2 10.4 %collective-permute-done.2.refs_1_.refs_2_ = f32[888,256]{1,0:T(8,128)S(1)} collective-permute-done((f32[888,256]{1,0:T(8,128)S(1)}, f32[888,256]{1,0:T(8,128)S(1)}, u32[]{:S(2)}, u32[]{:S(2)}) %collective-permute-start.2) | collective-permute-done | bytes 909344 | tf_op jit(solution)/shard_map/ppermute | solution.py:429
  76.0 4.6 %collective-permute-start.6 = (f32[696,256]{1,0:T(8,128)}, f32[696,256]{1,0:T(8,128)S(1)}, u32[]{:S(2)}, u32[]{:S(2)}) collective-permute-start(f32[696,256]{1,0:T(8,128)} %copy-done.18), channel_id=1, source_target_pairs={{0,4},{12,8},{1,5},{13,9},{2,6},{14,10},{3,7},{15,11},{16,20},{28,... | collective-permute-start | bytes 2138120 | tf_op jit(solution)/shard_map/ppermute | solution.py:429
  87.8 10.2 %shard_map.158 = (f32[2,1848,256]{2,1,0:T(8,128)}, f32[2,1848,256]{2,1,0:T(8,128)}, f32[8,128]{1,0:T(8,128)S(1)}) custom-call(bf16[7392,2048]{1,0:T(8,128)(2,1)} %bitcast.11, bf16[2048,256]{1,0:T(8,128)(2,1)S(1)} %pad_maximum_fusion.refs_1_, f32[8,128]{1,0:T(8,128)S(1)} %get-tuple-element.143.refs_2_), custom_call_target="tpu_custom_call" | custom-call | flops 1000000000 | bytes 10000000 | tf_op jit(solution)/shard_map/pallas_call | solution.py:80
  101.9 4.6 %collective-permute-start.11 = (f32[696,256]{1,0:T(8,128)S(1)}, f32[696,256]{1,0:T(8,128)S(1)}, u32[]{:S(2)}, u32[]{:S(2)}) collective-permute-start(f32[696,256]{1,0:T(8,128)S(1)} %get-tuple-element.150), channel_id=1, source_target_pairs={{0,4},{12,8},{1,5},{13,9},{2,6},{14,10},{3,7},{15,11},{16,20},{28,... | collective-permute-start | bytes 2138120 | tf_op jit(solution)/shard_map/ppermute | solution.py:429
  107.4 3.3 %shard_map.162 = (f32[1024,256]{1,0:T(8,128)S(1)}, f32[8,128]{1,0:T(8,128)S(1)}) custom-call(bf16[2048,2048]{1,0:T(8,128)(2,1)} %refs_0_.13, bf16[2048,256]{1,0:T(8,128)(2,1)} %refs_1_.13, f32[8,128]{1,0:T(8,128)S(1)} %get-tuple-element.151.refs_2_), custom_call_target="tpu_custom_call" | custom-call | flops 1000000000 | bytes 10000000 | tf_op jit(solution)/shard_map/pallas_call | solution.py:80
  111.2 10.2 %shard_map.164 = (f32[2,1848,256]{2,1,0:T(8,128)}, f32[2,1848,256]{2,1,0:T(8,128)}, f32[8,128]{1,0:T(8,128)S(1)}) custom-call(bf16[7392,2048]{1,0:T(8,128)(2,1)} %bitcast.12, bf16[2048,256]{1,0:T(8,128)(2,1)S(1)} %pad_maximum_fusion.refs_1_, f32[2,1848,256]{2,1,0:T(8,128)} %get-tuple-element.155.refs_2_, ...), custom_call_target="tpu_custom_call", output_to_operand_aliasing={{0}: (2, {}), {1}: (3, {})} | custom-call | flops 1000000000 | bytes 10000000 | tf_op jit(solution)/shard_map/pallas_call | solution.py:80
  127.9 4.6 %collective-permute-start.16 = (f32[696,256]{1,0:T(8,128)S(1)}, f32[696,256]{1,0:T(8,128)S(1)}, u32[]{:S(2)}, u32[]{:S(2)}) collective-permute-start(f32[696,256]{1,0:T(8,128)S(1)} %copy-done.17), channel_id=1, source_target_pairs={{0,4},{12,8},{1,5},{13,9},{2,6},{14,10},{3,7},{15,11},{16,20},{28,... | collective-permute-start | bytes 2138120 | tf_op jit(solution)/shard_map/ppermute | solution.py:429
  133.3 9.4 %collective-permute-done.14 = bf16[1024,256]{1,0:T(8,128)(2,1)S(1)} collective-permute-done((bf16[1024,256]{1,0:T(8,128)(2,1)S(1)}, bf16[1024,256]{1,0:T(8,128)(2,1)S(1)}, u32[]{:S(2)}, u32[]{:S(2)}) %collective-permute-start.14) | collective-permute-done | bytes 524320 | tf_op jit(solution)/shard_map/ppermute | solution.py:437
  143.8 6.3 %shard_map.171 = (f32[2,512,256]{2,1,0:T(8,128)}, f32[2,512,256]{2,1,0:T(8,128)}, f32[8,128]{1,0:T(8,128)S(1)}) custom-call(bf16[2048,2048]{1,0:T(8,128)(2,1)} %refs_0_.12, bf16[2048,256]{1,0:T(8,128)(2,1)} %pad_maximum_fusion.1.refs_1_, f32[8,128]{1,0:T(8,128)S(1)} %get-tuple-element.168.refs_2_), custom_call_target="tpu_custom_call" | custom-call | flops 1000000000 | bytes 10000000 | tf_op jit(solution)/shard_map/pallas_call | solution.py:80
  166.4 4.5 %collective-permute-done.20 = bf16[1024,256]{1,0:T(8,128)(2,1)S(1)} collective-permute-done((bf16[1024,256]{1,0:T(8,128)(2,1)S(1)}, bf16[1024,256]{1,0:T(8,128)(2,1)S(1)}, u32[]{:S(2)}, u32[]{:S(2)}) %collective-permute-start.20) | collective-permute-done | bytes 524320 | tf_op jit(solution)/shard_map/ppermute | solution.py:437
  171.5 15.8 %collective-permute-done.22 = bf16[1024,256]{1,0:T(8,128)(2,1)S(1)} collective-permute-done((bf16[1024,256]{1,0:T(8,128)(2,1)S(1)}, bf16[1024,256]{1,0:T(8,128)(2,1)S(1)}, u32[]{:S(2)}, u32[]{:S(2)}) %collective-permute-start.22) | collective-permute-done | bytes 524320 | tf_op jit(solution)/shard_map/ppermute | solution.py:437
  188.4 6.0 %shard_map.178 = (f32[2,512,256]{2,1,0:T(8,128)S(1)}, f32[2,512,256]{2,1,0:T(8,128)}, f32[8,128]{1,0:T(8,128)S(1)}) custom-call(bf16[2048,2048]{1,0:T(8,128)(2,1)} %refs_0_.13, bf16[2048,256]{1,0:T(8,128)(2,1)} %pad_maximum_fusion.2.refs_1_, f32[8,128]{1,0:T(8,128)S(1)} %get-tuple-element.189.refs_2_, f32[768,256]{1,0:T(8,128)S(1)} %pad_maximum_fusion.3.refs_3_.refs_2_), custom_call_target="tpu_custom_call" | custom-call | flops 1000000000 | bytes 10000000 | tf_op jit(solution)/shard_map/pallas_call | solution.py:80
  195.9 5.9 %collective-permute-done.24.refs_4_ = f32[1240,256]{1,0:T(8,128)S(1)} collective-permute-done((f32[1240,256]{1,0:T(8,128)S(1)}, f32[1240,256]{1,0:T(8,128)S(1)}, u32[]{:S(2)}, u32[]{:S(2)}) %collective-permute-start.24) | collective-permute-done | bytes 1269792 | tf_op jit(solution)/shard_map/ppermute | solution.py:465
  205.6 4.2 %collective-permute-done.19.refs_4_ = f32[360,256]{1,0:T(8,128)S(1)} collective-permute-done((f32[360,256]{1,0:T(8,128)S(1)}, f32[360,256]{1,0:T(8,128)S(1)}, u32[]{:S(2)}, u32[]{:S(2)}) %collective-permute-start.19) | collective-permute-done | bytes 368672 | tf_op jit(solution)/shard_map/ppermute | solution.py:465
  211.1 4.9 %collective-permute-done.25.refs_4_ = f32[360,256]{1,0:T(8,128)S(1)} collective-permute-done((f32[360,256]{1,0:T(8,128)S(1)}, f32[360,256]{1,0:T(8,128)S(1)}, u32[]{:S(2)}, u32[]{:S(2)}) %collective-permute-start.25) | collective-permute-done | bytes 368672 | tf_op jit(solution)/shard_map/ppermute | solution.py:465
  (158 shorter events, 62.4 us)
Async XLA Ops:
  9.6 20.1 %collective-permute-start = (f32[696,256]{1,0:T(8,128)S(1)}, f32[696,256]{1,0:T(8,128)S(1)}, u32[]{:S(2)}, u32[]{:S(2)}) collective-permute-start(f32[696,256]{1,0:T(8,128)S(1)} %get-tuple-element.105), channel_id=1, source_target_pairs={{0,4},{12,8},{1,5},{13,9},{2,6},{14,10},{3,7},{15,11},{16,20},{28,... | collective-permute-start | bytes 2138120 | tf_op jit(solution)/shard_map/ppermute | solution.py:429
  29.8 18.7 %collective-permute-start.1 = (f32[696,256]{1,0:T(8,128)S(1)}, f32[696,256]{1,0:T(8,128)S(1)}, u32[]{:S(2)}, u32[]{:S(2)}) collective-permute-start(f32[696,256]{1,0:T(8,128)S(1)} %get-tuple-element.119), channel_id=1, source_target_pairs={{0,4},{12,8},{1,5},{13,9},{2,6},{14,10},{3,7},{15,11},{16,20},{28,... | collective-permute-start | bytes 2138120 | tf_op jit(solution)/shard_map/ppermute | solution.py:429
  36.0 18.4 %collective-permute-start.3 = (f32[696,256]{1,0:T(8,128)S(1)}, f32[696,256]{1,0:T(8,128)S(1)}, u32[]{:S(2)}, u32[]{:S(2)}) collective-permute-start(f32[696,256]{1,0:T(8,128)S(1)} %get-tuple-element.122), channel_id=1, source_target_pairs={{4,8},{8,4},{5,9},{9,5},{6,10},{10,6},{7,11},{11,7},{20,24},{24,20... | collective-permute-start | bytes 2138120 | tf_op jit(solution)/shard_map/ppermute | solution.py:433
  48.5 22.0 %collective-permute-start.2 = (f32[888,256]{1,0:T(8,128)S(1)}, f32[888,256]{1,0:T(8,128)S(1)}, u32[]{:S(2)}, u32[]{:S(2)}) collective-permute-start(f32[888,256]{1,0:T(8,128)S(1)} %get-tuple-element.120), channel_id=1, source_target_pairs={{0,4},{12,8},{1,5},{13,9},{2,6},{14,10},{3,7},{15,11},{16,20},{28,... | collective-permute-start | bytes 2727944 | tf_op jit(solution)/shard_map/ppermute | solution.py:429
  53.7 18.6 %collective-permute-start.7 = (f32[696,256]{1,0:T(8,128)S(1)}, f32[696,256]{1,0:T(8,128)S(1)}, u32[]{:S(2)}, u32[]{:S(2)}) collective-permute-start(f32[696,256]{1,0:T(8,128)S(1)} %get-tuple-element.136), channel_id=1, source_target_pairs={{4,8},{8,4},{5,9},{9,5},{6,10},{10,6},{7,11},{11,7},{20,24},{24,20... | collective-permute-start | bytes 2138120 | tf_op jit(solution)/shard_map/ppermute | solution.py:433
  54.9 17.4 %collective-permute-start.5 = (bf16[1024,256]{1,0:T(8,128)(2,1)S(1)}, bf16[1024,256]{1,0:T(8,128)(2,1)S(1)}, u32[]{:S(2)}, u32[]{:S(2)}) collective-permute-start(bf16[1024,256]{1,0:T(8,128)(2,1)S(1)} %get-tuple-element.133), channel_id=1, source_target_pairs={{4,0},{8,12},{5,1},{9,13},{6,2},{10,14},{7,3},{11,15},{20,16},{24,... | collective-permute-start | bytes 1572872 | tf_op jit(solution)/shard_map/ppermute | solution.py:437
  74.7 13.0 %collective-permute-start.8 = (bf16[1024,256]{1,0:T(8,128)(2,1)S(1)}, bf16[1024,256]{1,0:T(8,128)(2,1)S(1)}, u32[]{:S(2)}, u32[]{:S(2)}) collective-permute-start(bf16[1024,256]{1,0:T(8,128)(2,1)S(1)} %get-tuple-element.142), channel_id=1, source_target_pairs={{4,0},{8,12},{5,1},{9,13},{6,2},{10,14},{7,3},{11,15},{20,16},{24,... | collective-permute-start | bytes 1572872 | tf_op jit(solution)/shard_map/ppermute | solution.py:437
  76.0 22.0 %collective-permute-start.6 = (f32[696,256]{1,0:T(8,128)}, f32[696,256]{1,0:T(8,128)S(1)}, u32[]{:S(2)}, u32[]{:S(2)}) collective-permute-start(f32[696,256]{1,0:T(8,128)} %copy-done.18), channel_id=1, source_target_pairs={{0,4},{12,8},{1,5},{13,9},{2,6},{14,10},{3,7},{15,11},{16,20},{28,... | collective-permute-start | bytes 2138120 | tf_op jit(solution)/shard_map/ppermute | solution.py:429
  80.7 19.3 %collective-permute-start.4 = (f32[888,256]{1,0:T(8,128)}, f32[888,256]{1,0:T(8,128)S(1)}, u32[]{:S(2)}, u32[]{:S(2)}) collective-permute-start(f32[888,256]{1,0:T(8,128)} %copy-done.13), channel_id=1, source_target_pairs={{4,8},{8,4},{5,9},{9,5},{6,10},{10,6},{7,11},{11,7},{20,24},{24,20... | collective-permute-start | bytes 2727944 | tf_op jit(solution)/shard_map/ppermute | solution.py:433
  100.6 20.8 %collective-permute-start.9 = (bf16[1408,256]{1,0:T(8,128)(2,1)S(1)}, bf16[1408,256]{1,0:T(8,128)(2,1)S(1)}, u32[]{:S(2)}, u32[]{:S(2)}) collective-permute-start(bf16[1408,256]{1,0:T(8,128)(2,1)S(1)} %get-tuple-element.147), channel_id=1, source_target_pairs={{4,0},{8,12},{5,1},{9,13},{6,2},{10,14},{7,3},{11,15},{20,16},{24,... | collective-permute-start | bytes 2162696 | tf_op jit(solution)/shard_map/ppermute | solution.py:437
  101.9 19.5 %collective-permute-start.11 = (f32[696,256]{1,0:T(8,128)S(1)}, f32[696,256]{1,0:T(8,128)S(1)}, u32[]{:S(2)}, u32[]{:S(2)}) collective-permute-start(f32[696,256]{1,0:T(8,128)S(1)} %get-tuple-element.150), channel_id=1, source_target_pairs={{0,4},{12,8},{1,5},{13,9},{2,6},{14,10},{3,7},{15,11},{16,20},{28,... | collective-permute-start | bytes 2138120 | tf_op jit(solution)/shard_map/ppermute | solution.py:429
  106.5 16.7 %collective-permute-start.10 = (f32[696,256]{1,0:T(8,128)S(1)}, f32[696,256]{1,0:T(8,128)S(1)}, u32[]{:S(2)}, u32[]{:S(2)}) collective-permute-start(f32[696,256]{1,0:T(8,128)S(1)} %get-tuple-element.149), channel_id=1, source_target_pairs={{4,8},{8,4},{5,9},{9,5},{6,10},{10,6},{7,11},{11,7},{20,24},{24,20... | collective-permute-start | bytes 2138120 | tf_op jit(solution)/shard_map/ppermute | solution.py:433
  126.3 29.9 %collective-permute-start.18 = (f32[2,1848,256]{2,1,0:T(8,128)}, f32[2,1848,256]{2,1,0:T(8,128)}, u32[]{:S(2)}, u32[]{:S(2)}) collective-permute-start(f32[2,1848,256]{2,1,0:T(8,128)} %get-tuple-element.179), channel_id=1, source_target_pairs={{0,1},{1,0},{2,3},{3,2},{4,5},{5,4},{6,7},{7,6},{8,9},{9,8},{10,11... | collective-permute-start | bytes 11354120 | tf_op jit(solution)/shard_map/ppermute | solution.py:461
  126.5 16.2 %collective-permute-start.14 = (bf16[1024,256]{1,0:T(8,128)(2,1)S(1)}, bf16[1024,256]{1,0:T(8,128)(2,1)S(1)}, u32[]{:S(2)}, u32[]{:S(2)}) collective-permute-start(bf16[1024,256]{1,0:T(8,128)(2,1)S(1)} %get-tuple-element.165), channel_id=1, source_target_pairs={{4,0},{8,12},{5,1},{9,13},{6,2},{10,14},{7,3},{11,15},{20,16},{24,... | collective-permute-start | bytes 1572872 | tf_op jit(solution)/shard_map/ppermute | solution.py:437
  127.9 22.2 %collective-permute-start.16 = (f32[696,256]{1,0:T(8,128)S(1)}, f32[696,256]{1,0:T(8,128)S(1)}, u32[]{:S(2)}, u32[]{:S(2)}) collective-permute-start(f32[696,256]{1,0:T(8,128)S(1)} %copy-done.17), channel_id=1, source_target_pairs={{0,4},{12,8},{1,5},{13,9},{2,6},{14,10},{3,7},{15,11},{16,20},{28,... | collective-permute-start | bytes 2138120 | tf_op jit(solution)/shard_map/ppermute | solution.py:429
  132.6 18.4 %collective-permute-start.15 = (f32[696,256]{1,0:T(8,128)S(1)}, f32[696,256]{1,0:T(8,128)S(1)}, u32[]{:S(2)}, u32[]{:S(2)}) collective-permute-start(f32[696,256]{1,0:T(8,128)S(1)} %copy-done.15), channel_id=1, source_target_pairs={{4,8},{8,4},{5,9},{9,5},{6,10},{10,6},{7,11},{11,7},{20,24},{24,20... | collective-permute-start | bytes 2138120 | tf_op jit(solution)/shard_map/ppermute | solution.py:433
  151.9 11.1 %collective-permute-start.21 = (f32[696,256]{1,0:T(8,128)S(1)}, f32[696,256]{1,0:T(8,128)}, u32[]{:S(2)}, u32[]{:S(2)}) collective-permute-start(f32[696,256]{1,0:T(8,128)S(1)} %get-tuple-element.186), channel_id=1, source_target_pairs={{4,8},{8,4},{5,9},{9,5},{6,10},{10,6},{7,11},{11,7},{20,24},{24,20... | collective-permute-start | bytes 2138120 | tf_op jit(solution)/shard_map/ppermute | solution.py:433
  153.4 12.8 %collective-permute-start.13 = (f32[384,256]{1,0:T(8,128)S(1)}, f32[384,256]{1,0:T(8,128)S(1)}, u32[]{:S(2)}, u32[]{:S(2)}) collective-permute-start(f32[384,256]{1,0:T(8,128)S(1)} %get-tuple-element.164), channel_id=1, source_target_pairs={{0,2},{2,0},{1,3},{3,1},{4,6},{6,4},{5,7},{7,5},{8,10},{10,8},{9,1... | collective-permute-start | bytes 1179656 | tf_op jit(solution)/shard_map/ppermute | solution.py:471
  155.0 15.9 %collective-permute-start.20 = (bf16[1024,256]{1,0:T(8,128)(2,1)S(1)}, bf16[1024,256]{1,0:T(8,128)(2,1)S(1)}, u32[]{:S(2)}, u32[]{:S(2)}) collective-permute-start(bf16[1024,256]{1,0:T(8,128)(2,1)S(1)} %get-tuple-element.184), channel_id=1, source_target_pairs={{4,0},{8,12},{5,1},{9,13},{6,2},{10,14},{7,3},{11,15},{20,16},{24,... | collective-permute-start | bytes 1572872 | tf_op jit(solution)/shard_map/ppermute | solution.py:437
  164.6 22.6 %collective-permute-start.22 = (bf16[1024,256]{1,0:T(8,128)(2,1)S(1)}, bf16[1024,256]{1,0:T(8,128)(2,1)S(1)}, u32[]{:S(2)}, u32[]{:S(2)}) collective-permute-start(bf16[1024,256]{1,0:T(8,128)(2,1)S(1)} %get-tuple-element.188), channel_id=1, source_target_pairs={{4,0},{8,12},{5,1},{9,13},{6,2},{10,14},{7,3},{11,15},{20,16},{24,... | collective-permute-start | bytes 1572872 | tf_op jit(solution)/shard_map/ppermute | solution.py:437
  170.9 30.9 %collective-permute-start.24 = (f32[1240,256]{1,0:T(8,128)S(1)}, f32[1240,256]{1,0:T(8,128)S(1)}, u32[]{:S(2)}, u32[]{:S(2)}) collective-permute-start(f32[1240,256]{1,0:T(8,128)S(1)} %get-tuple-element.193), channel_id=1, source_target_pairs={{0,2},{2,0},{1,3},{3,1},{4,6},{6,4},{5,7},{7,5},{8,10},{10,8},{9,1... | collective-permute-start | bytes 3809288 | tf_op jit(solution)/shard_map/ppermute | solution.py:465
  194.4 10.2 %collective-permute-start.23 = (f32[2,512,256]{2,1,0:T(8,128)S(1)}, f32[2,512,256]{2,1,0:T(8,128)S(1)}, u32[]{:S(2)}, u32[]{:S(2)}) collective-permute-start(f32[2,512,256]{2,1,0:T(8,128)S(1)} %get-tuple-element.191), channel_id=1, source_target_pairs={{0,1},{1,0},{2,3},{3,2},{4,5},{5,4},{6,7},{7,6},{8,9},{9,8},{10,11... | collective-permute-start | bytes 3145736 | tf_op jit(solution)/shard_map/ppermute | solution.py:461
  194.4 15.3 %collective-permute-start.19 = (f32[360,256]{1,0:T(8,128)S(1)}, f32[360,256]{1,0:T(8,128)S(1)}, u32[]{:S(2)}, u32[]{:S(2)}) collective-permute-start(f32[360,256]{1,0:T(8,128)S(1)} %get-tuple-element.183), channel_id=1, source_target_pairs={{0,2},{2,0},{1,3},{3,1},{4,6},{6,4},{5,7},{7,5},{8,10},{10,8},{9,1... | collective-permute-start | bytes 1105928 | tf_op jit(solution)/shard_map/ppermute | solution.py:465
  205.0 11.0 %collective-permute-start.25 = (f32[360,256]{1,0:T(8,128)S(1)}, f32[360,256]{1,0:T(8,128)S(1)}, u32[]{:S(2)}, u32[]{:S(2)}) collective-permute-start(f32[360,256]{1,0:T(8,128)S(1)} %get-tuple-element.199), channel_id=1, source_target_pairs={{0,2},{2,0},{1,3},{3,1},{4,6},{6,4},{5,7},{7,5},{8,10},{10,8},{9,1... | collective-permute-start | bytes 1105928 | tf_op jit(solution)/shard_map/ppermute | solution.py:465
  (35 other events, 161.2 us)
